TPU v7x, 128 devices: a whole 4x4x4 slice. The times are simulated.
128 devices in a mesh: phase: 2 (over y_lo), dp: 64 (over z, y_hi, x, core).
Axes of the slice: x: 4, y: 4 (y_hi: 2, y_lo: 2; y = y_hi * 2 + y_lo), z: 4, core: 2. Of those that a mesh axis runs over, the one named last changes fastest.
Arguments:
- block_input: bfloat16 [2, 4096, 1536], P(None, 'dp'), may hold values from -6 to 6
- cotangent: bfloat16 [2, 4096, 1536], P(None, 'dp'), may hold values from -6 to 6
- segments: int32 [2, 64, 64], P(None, 'dp'), may hold values from 0 to 3, never falling along the last dimension, each value on 1 to 32 neighbouring positions
- routes: int32 [2, 4096, 6], P(None, 'dp'), may hold values from 0 to 63, all different within a row; in each aligned block of 64 rows (0 to 63, 64 to 127, ..., all dimensions but the last counted through in order) at most 7 rows name the same one
- in_proj: bfloat16 [1536, 6448], P(('phase', 'dp')), may hold values from -0.15625 to 0.15625
- conv_taps: bfloat16 [4, 3328], P(None, ('phase', 'dp')), may hold values from -3 to 3
- conv_bias: bfloat16 [3328], P(('phase', 'dp')), may hold values from -3 to 3
- step_bias: float32 [48], replicated, may hold values from -4 to -1
- decay_log: float32 [48], replicated, may hold values from 0 to 2.7
- skip_weight: float32 [48], replicated, may hold values from 0.5 to 1.5
- norm_gain: bfloat16 [3072], P(('phase', 'dp')), may hold values from 0.5 to 1.5
- out_proj: bfloat16 [3072, 1536], P(('phase', 'dp')), may hold values from -0.109375 to 0.109375
- query_proj: bfloat16 [1536, 1536], P(('phase', 'dp')), may hold values from -0.15625 to 0.15625
- key_value_projection: bfloat16 [1536, 1024], P(('phase', 'dp')), may hold values from -0.15625 to 0.15625
- attn_out_proj: bfloat16 [1536, 1536], P(('phase', 'dp')), may hold values from -0.4375 to 0.4375
- norm_gains: bfloat16 [2, 2, 1536], P('phase', None, 'dp'), may hold values from 0.5 to 1.5
- router: bfloat16 [2, 1536, 64], P('phase', 'dp'), may hold values from -0.078125 to 0.078125
- shared_in: bfloat16 [2, 1536, 2048], P('phase', 'dp'), may hold values from -0.15625 to 0.15625
- shared_out: bfloat16 [2, 1024, 1536], P('phase', 'dp'), may hold values from -0.1875 to 0.1875
- experts_in: bfloat16 [2, 64, 1536, 1024], P('phase', 'dp'), may hold values from -0.15625 to 0.15625
- experts_out: bfloat16 [2, 64, 512, 1536], P('phase', 'dp'), may hold values from -0.5 to 0.5
Outputs:
- phase_outputs: bfloat16 [2, 2, 4096, 1536], P('phase', None, 'dp')
- input_grads: float32 [2, 2, 4096, 1536], P('phase', None, 'dp')
- in_proj_grad: float32 [1536, 6448], P(('phase', 'dp'))
- conv_taps_grad: float32 [4, 3328], P(None, ('phase', 'dp'))
- conv_bias_grad: float32 [3328], P(('phase', 'dp'))
- step_bias_grad: float32 [48], replicated
- decay_log_grad: float32 [48], replicated
- skip_weight_grad: float32 [48], replicated
- norm_gain_grad: float32 [3072], P(('phase', 'dp'))
- out_proj_grad: float32 [3072, 1536], P(('phase', 'dp'))
- query_proj_grad: float32 [1536, 1536], P(('phase', 'dp'))
- keyval_proj_grad: float32 [1536, 1024], P(('phase', 'dp'))
- attn_out_proj_grad: float32 [1536, 1536], P(('phase', 'dp'))
- norm_gains_grad: float32 [2, 2, 1536], P('phase', None, 'dp')
- router_grad: float32 [2, 1536, 64], P('phase', 'dp')
- shared_in_grad: float32 [2, 1536, 2048], P('phase', 'dp')
- shared_out_grad: float32 [2, 1024, 1536], P('phase', 'dp')
- experts_in_grad: float32 [2, 64, 1536, 1024], P('phase', 'dp')
- experts_out_grad: float32 [2, 64, 512, 1536], P('phase', 'dp')
Inputs may be any that keep to these rules, and one draw needn't show every extreme that they name: `segments`: never falls along a sequence; each segment has at most 32 tokens. `routes`: in each aligned block of 64 rows (the tokens of one sequence) no expert is named more than 7 times, a bound that some block reaches.
All inputs are finite; a program needn't handle non-finite values.
Results may differ from a plain program's by a relative error of at most 0.03.
Values may be sent and summed in bfloat16 or wider, within the bound.
A program may use at most 512 MiB of HBM per device.

v0:
```python
import functools

import jax
import jax.numpy as jnp
from jax import lax
from jax.experimental import pallas as pl
from jax.experimental.pallas import tpu as pltpu
from jax.sharding import Mesh
from jax.sharding import PartitionSpec as P

H = 48
P_SIZE = 64
N = 128
KW = 4
QUERY_HEADS = 12
KEY_VALUE_HEADS = 4
HEAD_SIZE = 128
DI = 3072
CONVW = 3328
WIDTH = 1536
SEQ = 64
EXPERTS = 64
SLOTS = 8
PARTS = 8
HEADS_HERE = H // PARTS
INNER = DI // PARTS
IN_COLS = 1152
QKV_COLS = 640

SIZES = {"phase": 2, "zh": 2, "zl": 2, "yh": 2, "x": 4, "core": 2}
TEAM = ("phase", "zh", "zl")
HALF = ("phase", "zh")
QUAD = ("zh", "zl")
RANK = ("yh", "x", "core")
DP = ("zh", "zl", "yh", "x", "core")
ALL = ("phase", "zh", "zl", "yh", "x", "core")
MESH_ID = pl.DeviceIdType.MESH

eps = 1e-05
single = jnp.float32
brain = jnp.bfloat16


def place_of(axes, index):
    out = {}
    for name in reversed(axes):
        out[name] = lax.rem(index, SIZES[name])
        index = lax.div(index, SIZES[name])
    return out


def size_of(axes):
    total = 1
    for name in axes:
        total *= SIZES[name]
    return total


def my_place(axes):
    me = jnp.int32(0)
    for name in axes:
        me = me * SIZES[name] + lax.axis_index(name)
    return me


def greet(barrier, device):
    pl.semaphore_signal(barrier, inc=1, device_id=device, device_id_type=MESH_ID)


def send(source, target, send_sem, recv_sem, device):
    copy = pltpu.make_async_remote_copy(
        src_ref=source,
        dst_ref=target,
        send_sem=send_sem,
        recv_sem=recv_sem,
        device_id=device,
        device_id_type=MESH_ID,
    )
    copy.start()
    return copy


def team_copies(axes, modes, sources, targets, send_sem, recv_sem, own_sem):
    n = size_of(axes)
    me = my_place(axes)
    copies = []
    for k in range(1, n):
        peer = lax.rem(me + k, n)
        device = place_of(axes, peer)
        for item, mode in enumerate(modes):
            if mode in SIZES:
                continue
            source = sources[item].at[peer] if mode == "swap" else sources[item]
            copies.append(
                send(
                    source,
                    targets[item].at[me],
                    send_sem.at[item, k],
                    recv_sem.at[item, k],
                    device,
                )
            )
    for item, mode in enumerate(modes):
        slot = me
        source = sources[item] if mode == "gather" else sources[item].at[me]
        if mode in SIZES:
            slot = lax.axis_index(mode)
            source = sources[item].at[slot]
            copies.append(
                send(
                    sources[item].at[1 - slot],
                    targets[item].at[slot],
                    send_sem.at[item, 0],
                    recv_sem.at[item, 0],
                    {mode: 1 - slot},
                )
            )
        copy = pltpu.make_async_copy(source, targets[item].at[slot], own_sem.at[item])
        copy.start()
        copies.append(copy)
    return copies


def greet_team(barrier, axes):
    n = size_of(axes)
    me = my_place(axes)
    for k in range(1, n):
        greet(barrier, place_of(axes, lax.rem(me + k, n)))
    return n - 1


def exchange_kernel(axes, modes, *refs):
    count = len(modes)
    barrier = pltpu.get_barrier_semaphore()
    pl.semaphore_wait(barrier, greet_team(barrier, axes))
    copies = team_copies(axes, modes, refs[:count], refs[count : 2 * count], *refs[2 * count :])
    for copy in copies:
        copy.wait()


def received(axes, items):
    n = size_of(axes)
    return [
        jax.ShapeDtypeStruct(((n,) if mode == "gather" else ()) + array.shape, array.dtype)
        for array, mode in items
    ]


def call(kernel, arrays, shapes, scratch, number, name, microseconds):
    moved = sum(s.size * s.dtype.itemsize for s in shapes)
    return pl.pallas_call(
        kernel,
        out_shape=shapes,
        in_specs=[pl.BlockSpec(memory_space=pltpu.VMEM)] * len(arrays),
        out_specs=[pl.BlockSpec(memory_space=pltpu.VMEM)] * len(shapes),
        scratch_shapes=scratch,
        compiler_params=pltpu.CompilerParams(
            collective_id=number, has_side_effects=True, vmem_limit_bytes=48 << 20
        ),
        cost_estimate=pl.CostEstimate(
            flops=microseconds * 10**9, bytes_accessed=2 * moved, transcendentals=0
        ),
        name=name,
    )(*arrays)


def team_semaphores(axes, items):
    return [
        pltpu.SemaphoreType.DMA((len(items), size_of(axes))),
        pltpu.SemaphoreType.DMA((len(items), size_of(axes))),
        pltpu.SemaphoreType.DMA((len(items),)),
    ]


def exchange(items, axes, number, name):
    return call(
        functools.partial(exchange_kernel, axes, tuple(mode for _, mode in items)),
        [array for array, _ in items],
        received(axes, items),
        team_semaphores(axes, items),
        number,
        name,
        20,
    )


def rank_devices():
    yh, x, core = lax.axis_index("yh"), lax.axis_index("x"), lax.axis_index("core")
    across = [lax.rem(x + k, 4) for k in range(4)]
    out = []
    for dy in range(2):
        for dx in range(4):
            for dc in range(2):
                y_at = 1 - yh if dy else yh
                c_at = 1 - core if dc else core
                device = {"yh": y_at, "x": across[dx], "core": c_at}
                out.append((device, y_at * 8 + across[dx] * 2 + c_at))
    return out


def for_each_expert_place(action):
    z = lax.axis_index("zh") * 2 + lax.axis_index("zl")
    rank = rank_devices()

    def of_layer(layer, own):
        high, low = lax.div(layer, 2), lax.rem(layer, 2)
        for k, (device, at) in enumerate(rank):
            action(dict(device, zh=high, zl=low), layer * 16 + at, own and k == 0)

    of_layer(z, True)

    def step(k, carry):
        of_layer(lax.rem(z + k, 4), False)
        return carry

    lax.fori_loop(1, 4, step, 0)


def expert_exchange_kernel(count, modes, *refs):
    every = count + len(modes)
    sources, targets = refs[:every], refs[every : 2 * every]
    send_sem, recv_sem, own_sem, rows_sent, rows_got = refs[2 * every :]
    mine = my_place(DP)
    barrier = pltpu.get_barrier_semaphore()

    def welcome(device, at, own):
        if not own:
            greet(barrier, device)

    for_each_expert_place(welcome)
    pl.semaphore_wait(barrier, 63)
    team = team_copies(
        QUAD, modes, sources[count:], targets[count:], send_sem, recv_sem, own_sem
    )

    def give(device, at, own):
        for item in range(count):
            source, target = sources[item].at[at], targets[item].at[mine]
            if own:
                pltpu.make_async_copy(source, target, rows_got.at[item]).start()
            else:
                send(source, target, rows_sent.at[item], rows_got.at[item], device)

    for_each_expert_place(give)
    for item in range(count):
        sent = sources[item].at[pl.ds(0, 63)]
        pltpu.make_async_copy(sent, sent, rows_sent.at[item]).wait()
        pltpu.make_async_copy(targets[item], targets[item], rows_got.at[item]).wait()
    for copy in team:
        copy.wait()


def expert_exchange(rows, items, number, name):
    rows = [value.reshape(EXPERTS, SLOTS, WIDTH) for value in rows]
    count = len(rows)
    out = call(
        functools.partial(expert_exchange_kernel, count, tuple(mode for _, mode in items)),
        rows + [array for array, _ in items],
        [jax.ShapeDtypeStruct(value.shape, brain) for value in rows] + received(QUAD, items),
        team_semaphores(QUAD, items)
        + [pltpu.SemaphoreType.DMA((count,)), pltpu.SemaphoreType.DMA((count,))],
        number,
        name,
        40 * count,
    )
    rows_got = [value.reshape(EXPERTS * SLOTS, WIDTH) for value in out[:count]]
    return rows_got + list(out[count:])


def rank_gather_kernel(count, modes, *refs):
    every = count + len(modes)
    sources, targets = refs[:count], refs[every : every + count]
    team_sources, team_targets = refs[count:every], refs[every + count : 2 * every]
    send_sem, recv_sem, own_sem, *team_sems = refs[2 * every :]
    yh, x, core = lax.axis_index("yh"), lax.axis_index("x"), lax.axis_index("core")
    right, left, far = lax.rem(x + 1, 4), lax.rem(x + 3, 4), lax.rem(x + 2, 4)
    other = 1 - yh
    to_y, to_right, to_left, to_core = {"yh": other}, {"x": right}, {"x": left}, {"core": 1 - core}
    barrier = pltpu.get_barrier_semaphore()
    for device in (to_y, to_right, to_left, to_core):
        greet(barrier, device)
    pl.semaphore_wait(barrier, 4 + greet_team(barrier, TEAM))

    def slot(y_at, x_at):
        return y_at * 8 + x_at * 2 + core

    sent = []

    def pass_on(item, at, kind, device, source=None):
        target = targets[item].at[at]
        copy = send(
            target if source is None else source,
            target,
            send_sem.at[item, kind],
            recv_sem.at[item, kind],
            device,
        )
        sent.append(copy)
        return copy

    def arrived(item, kind):
        pltpu.make_async_copy(sources[item], sources[item], recv_sem.at[item, kind]).wait()

    items = range(count)
    me = slot(yh, x)
    own = []
    for item in items:
        pass_on(item, me, 0, to_y, sources[item])
        pass_on(item, me, 1, to_right, sources[item])
        pass_on(item, me, 2, to_left, sources[item])
        pass_on(item, me, 7, to_core, sources[item])
        copy = pltpu.make_async_copy(sources[item], targets[item].at[me], own_sem.at[item])
        copy.start()
        own.append(copy)
    team = team_copies(TEAM, modes, team_sources, team_targets, *team_sems)
    steps = (
        (1, slot(yh, left), ((5, to_right), (8, to_core))),
        (0, slot(other, x), ((3, to_right), (4, to_left), (9, to_core))),
        (2, slot(yh, right), ((10, to_core),)),
        (4, slot(other, right), ((6, to_left), (11, to_core))),
        (3, slot(other, left), ((12, to_core),)),
        (5, slot(yh, far), ((13, to_core),)),
        (6, slot(other, far), ((14, to_core),)),
    )
    for kind, at, onward in steps:
        for item in items:
            arrived(item, kind)
            for next_kind, device in onward:
                pass_on(item, at, next_kind, device)
    for item in items:
        for kind in range(7, 15):
            arrived(item, kind)
    for copy in own:
        copy.wait()
    for copy in sent:
        copy.wait_send()
    for copy in team:
        copy.wait()


def rank_gather(arrays, items, number, name):
    count = len(arrays)
    return call(
        functools.partial(rank_gather_kernel, count, tuple(mode for _, mode in items)),
        arrays + [array for array, _ in items],
        [jax.ShapeDtypeStruct((16,) + array.shape, array.dtype) for array in arrays]
        + received(TEAM, items),
        [
            pltpu.SemaphoreType.DMA((count, 15)),
            pltpu.SemaphoreType.DMA((count, 15)),
            pltpu.SemaphoreType.DMA((count,)),
        ]
        + team_semaphores(TEAM, items),
        number,
        name,
        40,
    )


def rank_sum_kernel(count, extra, *refs):
    every = count + extra
    sources, given = refs[:count], refs[count:every]
    targets, taken = refs[every : every + count], refs[every + count : 2 * every]
    refs = refs[2 * every :]
    from_core, totals, arrivals = (refs[k * count : (k + 1) * count] for k in range(3))
    send_sem, recv_sem, give_sem, take_sem = refs[3 * count :]
    yh, x, core = lax.axis_index("yh"), lax.axis_index("x"), lax.axis_index("core")
    right, left, far = lax.rem(x + 1, 4), lax.rem(x + 3, 4), lax.rem(x + 2, 4)
    other = 1 - yh
    to_y, to_right, to_left, to_core = {"yh": other}, {"x": right}, {"x": left}, {"core": 1 - core}
    barrier = pltpu.get_barrier_semaphore()
    to_phase = {"phase": 1 - lax.axis_index("phase")}
    for device in (to_y, to_right, to_left, to_core, to_phase):
        greet(barrier, device)
    pl.semaphore_wait(barrier, 5)
    items = range(count)
    sent = []

    def pass_on(item, at, kind, device):
        copy = send(
            totals[item].at[at],
            arrivals[item].at[kind],
            send_sem.at[item, kind],
            recv_sem.at[item, kind],
            device,
        )
        sent.append(copy)

    def arrived(item, kind):
        landed = arrivals[item].at[kind]
        pltpu.make_async_copy(landed, landed, recv_sem.at[item, kind]).wait()
        return arrivals[item][kind].astype(single)

    def slot(y_at, x_at):
        return y_at * 4 + x_at

    for item in items:
        sent.append(
            send(
                sources[item].at[:, 1 - core],
                from_core[item],
                send_sem.at[item, 7],
                recv_sem.at[item, 7],
                to_core,
            )
        )
    swaps = [
        send(given[k], taken[k], give_sem.at[k], take_sem.at[k], to_phase) for k in range(extra)
    ]
    for item in items:
        landed = from_core[item]
        pltpu.make_async_copy(landed, landed, recv_sem.at[item, 7]).wait()

        def add(at):
            value = sources[item][at, core].astype(single) + from_core[item][at].astype(single)
            totals[item][at] = value.astype(brain)

        add(slot(yh, far))
        pass_on(item, slot(yh, far), 0, to_right)
        add(slot(other, far))
        pass_on(item, slot(other, far), 1, to_left)
        add(slot(other, right))
        pass_on(item, slot(other, right), 3, to_right)
        add(slot(yh, left))
        pass_on(item, slot(yh, left), 5, to_left)
        for at in (slot(yh, right), slot(other, left), slot(yh, x), slot(other, x)):
            add(at)
    for item in items:
        at = slot(yh, right)
        totals[item][at] = (totals[item][at].astype(single) + arrived(item, 0)).astype(brain)
        pass_on(item, at, 2, to_right)
        at = slot(other, left)
        totals[item][at] = (totals[item][at].astype(single) + arrived(item, 1)).astype(brain)
        pass_on(item, at, 4, to_left)
    for item in items:
        at = slot(other, x)
        value = totals[item][at].astype(single) + arrived(item, 3)
        totals[item][at] = (value + arrived(item, 4)).astype(brain)
        pass_on(item, at, 6, to_y)
    for item in items:
        value = totals[item][slot(yh, x)].astype(single) + arrived(item, 5)
        value = value + arrived(item, 2)
        targets[item][...] = (value + arrived(item, 6)).astype(targets[item].dtype)
    for copy in sent:
        copy.wait_send()
    for copy in swaps:
        copy.wait()


def rank_sum(arrays, swapped, number, name):
    count, extra = len(arrays), len(swapped)
    arrays = [array.reshape((8, 2) + array.shape[1:]) for array in arrays]
    pieces = [array.shape[2:] for array in arrays]
    scratch = [pltpu.VMEM((8,) + piece, brain) for piece in pieces]
    scratch += [pltpu.VMEM((8,) + piece, brain) for piece in pieces]
    scratch += [pltpu.VMEM((7,) + piece, brain) for piece in pieces]
    scratch += [pltpu.SemaphoreType.DMA((count, 8)), pltpu.SemaphoreType.DMA((count, 8))]
    scratch += [pltpu.SemaphoreType.DMA((extra,)), pltpu.SemaphoreType.DMA((extra,))]
    return call(
        functools.partial(rank_sum_kernel, count, extra),
        arrays + swapped,
        [jax.ShapeDtypeStruct(piece, brain) for piece in pieces]
        + [jax.ShapeDtypeStruct(array.shape, array.dtype) for array in swapped],
        scratch,
        number,
        name,
        45,
    )


def dot(left, right):
    return jnp.dot(left, right, preferred_element_type=single)


def dot_t(left, right):
    return lax.dot_general(left, right, (((1,), (1,)), ((), ())), preferred_element_type=single)


def t_dot(left, right):
    return lax.dot_general(left, right, (((0,), (0,)), ((), ())), preferred_element_type=single)


def exact(spec, left, right):
    return jnp.einsum(
        spec, left, right, precision=lax.Precision.HIGHEST, preferred_element_type=single
    )


def rms_scale(value, gain):
    return value * lax.rsqrt(jnp.mean(value * value, axis=-1, keepdims=True) + eps) * gain


def swiglu(value):
    half = value.shape[-1] // 2
    return jax.nn.silu(value[..., :half]) * value[..., half:]


def shuffle_matrix():
    to = jnp.arange(WIDTH, dtype=jnp.int32)
    origin = to // 12 % 8 * 192 + to // 96 * 12 + to % 12
    return (jnp.arange(WIDTH, dtype=jnp.int32)[:, None] == origin[None, :]).astype(brain)


def shuffle(value, matrix):
    return dot(value, matrix).astype(brain)


def unshuffle(value, matrix):
    high = value.astype(brain)
    lower = (value - high.astype(single)).astype(brain)
    both = dot_t(jnp.concatenate([high, lower], axis=0), matrix)
    return both[: value.shape[0]] + both[value.shape[0] :]


def after(values, first):
    return lax.optimization_barrier((values, first))[0]


def pad_rows(value, rows):
    return jnp.pad(value, [(0, 0)] * (value.ndim - 2) + [(0, rows - value.shape[-2]), (0, 0)])


def pad_to(value, rows, columns):
    return jnp.pad(value, ((0, rows - value.shape[0]), (0, columns - value.shape[1])))


def allowed_pairs(seg):
    position = jnp.arange(SEQ, dtype=jnp.int32)
    return (position[:, None] >= position[None, :]) & (seg[..., :, None] == seg[..., None, :])


def product(left, right, dims, precision=None):
    return lax.dot_general(
        left, right, (dims, ((), ())), precision=precision, preferred_element_type=single
    )


def sharp(left, right, dims):
    return product(left, right, dims, lax.Precision.HIGHEST)


def blunt(left, right, dims):
    return product(left.astype(brain), right.astype(brain), dims)


def mamba_parts(zx_ref, masks_ref, same_ref, taps_ref, heads_ref):
    zx = zx_ref[0]
    conv_in = zx[:, INNER : 2 * INNER + 2 * N]
    taps = taps_ref[...]
    same = same_ref[0]
    moved = [conv_in]
    for k in range(1, KW):
        moved.append(pltpu.roll(conv_in, k, 0) * same[:, k : k + 1])
    conv = taps[KW : KW + 1]
    for k in range(KW):
        conv = conv + taps[KW - 1 - k : KW - k] * moved[k]
    gate = jax.nn.sigmoid(conv)
    active = conv * gate
    heads = heads_ref[...]
    raw = zx[:, 2 * INNER + 2 * N :] + heads[0:1]
    step = jnp.maximum(raw, 0.0) + jnp.log1p(jnp.exp(-jnp.abs(raw)))
    rate = step * heads[1:2]
    rows = lax.broadcasted_iota(jnp.int32, (SEQ, SEQ), 0)
    columns = lax.broadcasted_iota(jnp.int32, (SEQ, SEQ), 1)
    lower = (rows >= columns).astype(single)
    total = sharp(lower, rate, ((1,), (0,)))
    total_t = sharp(rate, lower, ((0,), (1,)))
    unit = (rows == columns).astype(single)
    step_t = sharp(step, unit, ((0,), (1,)))
    values = active[:, :INNER]
    in_state, out_state = active[:, INNER : INNER + N], active[:, INNER + N :]
    meeting = sharp(out_state, in_state, ((1,), (1,)))
    allowed = masks_ref[0]
    decays = []
    results = []
    for h in range(HEADS_HERE):
        fall = jnp.exp(jnp.minimum(total[:, h : h + 1] - total_t[h : h + 1], 0.0)) * allowed
        mixing = fall * meeting * step_t[h : h + 1]
        decays.append((fall, mixing))
        results.append(blunt(mixing, values[:, h * P_SIZE : (h + 1) * P_SIZE], ((1,), (0,))))
    result = jnp.concatenate(results, axis=1) + taps[5:6, :INNER] * values
    z = zx[:, :INNER]
    open_z = jax.nn.sigmoid(z)
    return (
        (zx, taps, same, moved, conv, gate, heads, raw, step, step_t, unit, lower),
        (values, in_state, out_state, meeting, decays, result, z, open_z),
    )


def mamba_forward_kernel(zx_ref, masks_ref, same_ref, taps_ref, heads_ref, part_ref, squares_ref):
    (_, taps, *_), (*_, result, z, open_z) = mamba_parts(
        zx_ref, masks_ref, same_ref, taps_ref, heads_ref
    )
    gated = result * (z * open_z)
    part_ref[0] = (gated * taps[6:7, :INNER]).astype(brain)
    sums = sharp(jnp.ones((8, INNER), single), gated * gated, ((1,), (1,)))
    squares_ref[0] = jnp.concatenate([sums, jnp.zeros((8, 128 - SEQ), single)], axis=1)


def mamba_backward_kernel(
    zx_ref, masks_ref, same_ref, taps_ref, heads_ref, d_yn_ref, scalars_ref, d_zx_ref, yn_ref, sums_ref
):
    first, second = mamba_parts(zx_ref, masks_ref, same_ref, taps_ref, heads_ref)
    (zx, taps, same, moved, conv, gate, heads, raw, step, step_t, unit, lower) = first
    (values, in_state, out_state, meeting, decays, result, z, open_z) = second
    scalars = sharp(unit, scalars_ref[0][:, :SEQ], ((1,), (1,)))
    inverse, along = scalars[:, 0:1], scalars[:, 1:2]
    gain, skip = taps[6:7, :INNER], taps[5:6, :INNER]
    d_yn = d_yn_ref[0]
    shut = z * open_z
    gated = result * shut
    scaled = gated * inverse
    yn_ref[0] = (scaled * gain).astype(brain)
    d_gain = jnp.sum(d_yn * scaled, axis=0, keepdims=True)
    d_gated = inverse * gain * d_yn - gated * along
    d_z = d_gated * result * (open_z * (1.0 + z * (1.0 - open_z)))
    d_result = d_gated * shut
    d_skip = jnp.sum(d_result * values, axis=0, keepdims=True)
    lanes = lax.broadcasted_iota(jnp.int32, (1, 128), 1)
    rows = lax.broadcasted_iota(jnp.int32, (128, 1), 0)
    d_meeting = jnp.zeros((SEQ, SEQ), single)
    by_row = jnp.zeros((SEQ, 128), single)
    by_column = jnp.zeros((128, SEQ), single)
    d_step_t = jnp.zeros((128, SEQ), single)
    d_values = []
    for h in range(HEADS_HERE):
        fall, mixing = decays[h]
        own = slice(h * P_SIZE, (h + 1) * P_SIZE)
        d_mixing = blunt(d_result[:, own], values[:, own], ((1,), (1,)))
        d_values.append(blunt(mixing, d_result[:, own], ((0,), (0,))))
        spread = d_mixing * fall
        d_meeting = d_meeting + spread * step_t[h : h + 1]
        spread = spread * meeting
        moving = spread * step_t[h : h + 1]
        by_row = by_row + jnp.sum(moving, axis=1, keepdims=True) * (lanes == h).astype(single)
        at = (rows == h).astype(single)
        by_column = by_column + at * jnp.sum(moving, axis=0, keepdims=True)
        d_step_t = d_step_t + at * jnp.sum(spread, axis=0, keepdims=True)
    d_total = by_row - sharp(unit, by_column, ((1,), (1,)))
    d_rate = sharp(lower, d_total, ((0,), (0,)))
    d_step = sharp(unit, d_step_t, ((1,), (1,))) + d_rate * heads[1:2]
    d_raw = d_step * jax.nn.sigmoid(raw)
    d_decay = jnp.sum(d_rate * step, axis=0, keepdims=True) * heads[1:2]
    d_active = jnp.concatenate(
        [
            jnp.concatenate(d_values, axis=1) + skip * d_result,
            sharp(d_meeting, out_state, ((0,), (0,))),
            sharp(d_meeting, in_state, ((1,), (0,))),
        ],
        axis=1,
    )
    d_conv = d_active * (gate * (1.0 + conv * (1.0 - gate)))
    d_taps = [jnp.sum(d_conv * moved[KW - 1 - k], axis=0, keepdims=True) for k in range(KW)]
    d_in = taps[KW - 1 : KW] * d_conv
    for k in range(1, KW):
        d_in = d_in + pltpu.roll(
            taps[KW - 1 - k : KW - k] * (d_conv * same[:, k : k + 1]), SEQ - k, 0
        )
    d_zx_ref[0] = jnp.concatenate([d_z, d_in, d_raw], axis=1).astype(brain)
    wide = INNER + 2 * N

    def widen(value):
        return jnp.concatenate(
            [value, jnp.zeros((1, wide - value.shape[1]), single)], axis=1
        )

    sums = jnp.concatenate(
        d_taps
        + [jnp.sum(d_conv, axis=0, keepdims=True), widen(d_skip), widen(d_gain)]
        + [widen(jnp.sum(d_raw, axis=0, keepdims=True)), widen(d_decay)]
        + [jnp.zeros((7, wide), single)],
        axis=0,
    )

    @pl.when(pl.program_id(0) == 0)
    def _():
        sums_ref[...] = jnp.zeros_like(sums_ref)

    sums_ref[...] += sums


def by_sequence(kernel, arrays, fixed, shapes, total_shapes, name):
    def whole(shape):
        return pl.BlockSpec(shape, lambda n: (0,) * len(shape))

    def one(shape):
        return pl.BlockSpec((1,) + shape[1:], lambda n: (n,) + (0,) * (len(shape) - 1))

    return pl.pallas_call(
        kernel,
        grid=(PARTS,),
        out_shape=shapes + total_shapes,
        in_specs=[
            whole(array.shape) if place in fixed else one(array.shape)
            for place, array in enumerate(arrays)
        ],
        out_specs=[one(s.shape) for s in shapes] + [whole(s.shape) for s in total_shapes],
        compiler_params=pltpu.CompilerParams(vmem_limit_bytes=32 << 20),
        name=name,
    )(*arrays)


def attend_scores(queries, keys, seg):
    scores = exact("nird,njd->nrij", queries, keys) * HEAD_SIZE ** (-0.5)
    scores = jnp.where(allowed_pairs(seg)[:, None], scores, -1e30)
    return jax.nn.softmax(scores, axis=-1)


def attend_mix(probs, values):
    return exact("nrij,njd->nird", probs, values)


def per_device(
    block_input,
    cotangent,
    segments,
    routes,
    in_proj,
    conv_taps,
    conv_bias,
    step_bias,
    decay_log,
    skip_weight,
    norm_gain,
    out_proj,
    query_proj,
    key_value_projection,
    attn_out_proj,
    norm_gains,
    router,
    shared_in,
    shared_out,
    experts_in,
    experts_out,
):
    phase = lax.axis_index("phase")
    first_phase = phase == 0
    zl = lax.axis_index("zl")
    team = phase * 4 + lax.axis_index("zh") * 2 + zl

    def mine(value):
        return lax.dynamic_index_in_dim(value, phase, 0, keepdims=False)

    start = mine(block_input)
    cot = mine(cotangent)
    seg = mine(segments)
    route_rows = mine(routes)

    both_ways = [(0, 1), (1, 0)]
    w_first, w_second = experts_in[0, 0], experts_out[0, 0]

    z_piece = in_proj[:, :DI].reshape(12, PARTS, INNER).transpose(1, 0, 2)
    x_piece = in_proj[:, DI : 2 * DI].reshape(12, PARTS, INNER).transpose(1, 0, 2)
    state_piece = jnp.broadcast_to(in_proj[None, :, 2 * DI : 2 * DI + 2 * N], (PARTS, 12, 2 * N))
    step_piece = in_proj[:, 2 * DI + 2 * N :].reshape(12, PARTS, HEADS_HERE).transpose(1, 0, 2)
    step_piece = jnp.pad(step_piece, ((0, 0), (0, 0), (0, 128 - HEADS_HERE)))
    q_piece = query_proj.reshape(12, 4, 384).transpose(1, 0, 2)
    kv_piece = key_value_projection.reshape(12, 2, 4, 128).transpose(2, 0, 1, 3).reshape(4, 12, 256)
    qkv_piece = jnp.repeat(jnp.concatenate([q_piece, kv_piece], axis=2), 2, axis=0)
    in_piece = pad_rows(jnp.concatenate([z_piece, x_piece, state_piece, step_piece], axis=2), 16)
    qkv_piece = pad_rows(qkv_piece, 16)
    sin_piece = shared_in[0].reshape(24, 2, 4, 256).transpose(2, 0, 1, 3).reshape(4, 24, 512)
    sin_piece = pad_rows(jnp.concatenate([sin_piece, sin_piece], axis=0), 32)
    sout_piece = jnp.broadcast_to(shared_out, (2, 16, WIDTH))
    attn_piece = jnp.broadcast_to(pad_rows(attn_out_proj, 16)[None], (2, 16, WIDTH))
    mixing = shuffle_matrix()
    rest = jnp.concatenate(
        [conv_taps.reshape(-1), conv_bias, norm_gain, norm_gains[0].reshape(-1)]
    )
    rest = jnp.pad(rest, (0, 512 - rest.shape[0])).reshape(4, 128)
    small = jnp.concatenate([router[0].reshape(12, 128), rest], axis=0)
    seg_piece = pad_to(seg, 8, 128)
    in_got, sin_got, sout_got, small_got, seg_got = exchange(
        [
            (in_piece, "swap"),
            (sin_piece, "swap"),
            (sout_piece, "phase"),
            (small, "gather"),
            (seg_piece, "gather"),
        ],
        TEAM,
        0,
        "team_start",
    )
    seg_all = seg_got[:, 0, :SEQ]
    sin_got = sin_got[:, :24].reshape(2, 96, 512)
    w_in, small_all, w_out, sin_all, sout_all, start_all, qkv_got, attn_got = rank_gather(
        [
            in_got[:, :12].reshape(96, IN_COLS),
            small_got.reshape(128, 128),
            pad_rows(out_proj, 32),
            sin_got[0],
            sout_got[0],
        ],
        [(shuffle(start, mixing), "gather"), (qkv_piece, "swap"), (attn_piece, "zl")],
        1,
        "rank_weights",
    )
    w_in = w_in.reshape(WIDTH, IN_COLS)
    w_out = w_out[:, :24].reshape(INNER, WIDTH)
    later_wide = jnp.concatenate([qkv_got[:, :12].reshape(96, QKV_COLS), sin_got[1]], axis=1)
    later_tall = jnp.concatenate([attn_got[:, :12].reshape(24, WIDTH), sout_got[1]], axis=0)
    w_first_far = lax.ppermute(w_first, "phase", both_ways)
    w_second_far = lax.ppermute(w_second, "phase", both_ways)
    later_wide = lax.all_gather(later_wide, RANK, axis=0)
    later_tall = lax.all_gather(later_tall, RANK, axis=0)
    w_qkv = later_wide[:, :, :QKV_COLS].reshape(WIDTH, QKV_COLS)
    w_attn = later_tall[:, :24].reshape(16, 2, 12, WIDTH).transpose(1, 0, 2, 3)
    w_attn = w_attn.reshape(384, WIDTH)

    def hidden_in(value):
        return value.reshape(16, 4, 24, 512).transpose(1, 0, 2, 3).reshape(WIDTH, 512)

    sin_full = (hidden_in(sin_all), hidden_in(later_wide[:, :, QKV_COLS:]))
    sout_full = (sout_all.reshape(256, WIDTH), later_tall[:, 24:].reshape(256, WIDTH))
    small_all = small_all.reshape(16, 2, 4, 16, 128)
    router_full = small_all[:, :, :, :12].reshape(16, 2, 4, 24, EXPERTS).transpose(1, 2, 0, 3, 4)
    router_full = router_full.reshape(2, WIDTH, EXPERTS)
    rest_all = small_all[:, :, :, 12:].reshape(16, 2, 4, 512)
    conv_full = rest_all[..., :130].reshape(16, 2, 4, 5, 26).transpose(3, 1, 2, 0, 4)
    conv_full = conv_full.reshape(5, CONVW).astype(single)
    gain_here = rest_all[..., 130:154].reshape(16, 8, 24)
    gain_here = lax.dynamic_index_in_dim(gain_here, team, 1, keepdims=False)
    gain_here = gain_here.reshape(INNER).astype(single)
    gains = rest_all[..., 154:202].reshape(16, 2, 4, 2, 24).transpose(1, 3, 2, 0, 4)
    gains = gains.reshape(2, 2, WIDTH).astype(single)
    conv_here = jnp.concatenate(
        [lax.dynamic_slice_in_dim(conv_full[:, :DI], team * INNER, INNER, 1), conv_full[:, DI:]],
        axis=1,
    )

    def heads_of(value):
        return lax.dynamic_slice_in_dim(value, team * HEADS_HERE, HEADS_HERE, 0)

    skip_wide = jnp.repeat(heads_of(skip_weight), P_SIZE)
    columns = jnp.stack([jnp.pad(skip_wide, (0, 2 * N)), jnp.pad(gain_here, (0, 2 * N))])
    taps_here = jnp.concatenate([conv_here, columns, jnp.zeros((1, INNER + 2 * N), single)], axis=0)
    heads_here = jnp.stack([heads_of(step_bias), -jnp.exp(heads_of(decay_log))])
    heads_here = pad_to(heads_here, 8, 128)
    allowed_all = allowed_pairs(seg_all).astype(single)
    same_all = [
        jnp.pad(seg_all[:, k:] == seg_all[:, : SEQ - k], ((0, 0), (k, 0))) for k in range(KW)
    ]
    same_all = jnp.pad(jnp.stack(same_all, axis=2).astype(single), ((0, 0), (0, 0), (0, 128 - KW)))

    expert_ids = jnp.arange(EXPERTS, dtype=jnp.int32)
    named = jnp.any(route_rows[:, :, None] == expert_ids, axis=1)
    position = jnp.arange(SEQ, dtype=jnp.int32)
    earlier = (position[:, None] > position[None, :]).astype(brain)
    slot = dot(earlier, named.astype(brain))
    slot = jnp.where(named, slot, -1.0).astype(brain)
    cell = jnp.arange(EXPERTS * SLOTS, dtype=jnp.int32)
    spread = (cell[None, :] // SLOTS == expert_ids[:, None]).astype(brain)
    taken = dot(slot, spread) == (cell % SLOTS).astype(single)
    taken_b = taken.astype(brain)

    def of_block(s):
        own = phase == s
        return (
            jnp.where(own, w_first, w_first_far),
            jnp.where(own, w_second, w_second_far),
        )

    def moe_open(s, hidden):
        normed = rms_scale(hidden, gains[s, 1]).astype(brain)
        logits = dot(normed, router_full[s])
        top = jnp.max(jnp.where(named, logits, -jnp.inf), axis=1, keepdims=True)
        weight = jnp.where(named, jnp.exp(logits - top), 0.0)
        gates = weight / jnp.sum(weight, axis=1, keepdims=True)
        gates_wide = jnp.where(taken, exact("ie,ec->ic", gates, spread.astype(single)), 0.0)
        return normed, gates, gates_wide, t_dot(taken_b, normed).astype(brain)

    def moe_experts(weights, rows_in):
        both = dot(rows_in, weights[0])
        hid = swiglu(both).astype(brain)
        return both, hid, dot(hid, weights[1]).astype(brain)

    def moe_shared(s, normed_all):
        both = dot(normed_all, sin_full[s])
        hid = swiglu(both).astype(brain)
        part = dot(hid, sout_full[s]).astype(brain)
        return both, hid, part.reshape(4, SEQ, WIDTH)

    def moe_join(hidden, gates_wide, back, shared_got):
        high = gates_wide.astype(brain)
        lower = (gates_wide - high.astype(single)).astype(brain)
        moe = dot(high, back) + dot(lower, back)
        return (hidden + moe + jnp.sum(shared_got.astype(single), axis=0)).astype(brain)

    def back_open(d_out, gates_wide):
        gate_cell = jnp.sum(gates_wide, axis=0)
        return (t_dot(taken_b, d_out) * gate_cell[:, None]).astype(brain)

    def back_experts(weights, d_answer, both):
        d_hid = dot_t(d_answer, weights[1])
        d_both = jax.vjp(swiglu, both)[1](d_hid)[0].astype(brain)
        return d_both, dot_t(d_both, weights[0]).astype(brain)

    def back_shared(s, d_out_all, normed_all, both, hid):
        d_hid = dot_t(d_out_all, sout_full[s])
        d_sout = t_dot(hid, d_out_all)
        d_both = jax.vjp(swiglu, both)[1](d_hid)[0].astype(brain)
        d_sin = t_dot(normed_all, d_both)
        d_part = dot_t(d_both, sin_full[s]).astype(brain).reshape(4, SEQ, WIDTH)
        return d_sin, d_sout, d_part

    def back_join(s, d_out, hidden, normed, gates, back, returned, d_shared_got):
        d_cells = jnp.where(taken, dot_t(d_out, back), 0.0)
        d_gates = exact("ic,ec->ie", d_cells, spread.astype(single))
        d_logits = gates * (d_gates - jnp.sum(gates * d_gates, axis=1, keepdims=True))
        d_normed = exact("ie,we->iw", d_logits, router_full[s].astype(single))
        d_router = exact("iw,ie->we", normed.astype(single), d_logits)
        d_normed = d_normed + dot(taken_b, returned) + jnp.sum(d_shared_got.astype(single), axis=0)
        d_hidden, d_gain = jax.vjp(rms_scale, hidden, gains[s, 1])[1](d_normed)
        return d_hidden + d_out.astype(single), d_gain, d_router

    def shared_in_parts(value):
        return value.astype(brain).reshape(4, 16, 24, 512).transpose(1, 0, 2, 3).reshape(16, 96, 512)

    u0 = start.astype(single)
    shuffled_gain = shuffle(gains[0, 0][None].astype(brain), mixing)[0].astype(single)
    n1_all = rms_scale(start_all.astype(single), shuffled_gain).astype(brain)
    n1_all = n1_all.reshape(PARTS * SEQ, WIDTH)
    zx = dot(n1_all, w_in).reshape(PARTS, SEQ, IN_COLS)

    core_inputs = [zx, allowed_all, same_all, taps_here, heads_here]
    part, squares = by_sequence(
        mamba_forward_kernel,
        core_inputs,
        (3, 4),
        [
            jax.ShapeDtypeStruct((PARTS, SEQ, INNER), brain),
            jax.ShapeDtypeStruct((PARTS, 8, 128), single),
        ],
        [],
        "mamba_forward",
    )
    part = dot(part.reshape(PARTS * SEQ, INNER), w_out)
    part = part.astype(brain).reshape(PARTS, SEQ, WIDTH)
    part = after(part, (w_first_far, w_second_far))
    part_got, squares_got = exchange([(part, "swap"), (squares, "swap")], TEAM, 2, "team_mixed_0")
    mean_square = jnp.sum(squares_got[:, 0, :SEQ], axis=0) / DI
    inverse = lax.rsqrt(mean_square + eps)
    mixed0 = jnp.sum(part_got.astype(single), axis=0) * inverse[:, None]
    hidden0 = u0 + mixed0
    normed0, gates0, gates_wide0, rows_out0 = moe_open(0, hidden0)
    rows_in0, normed_all0 = expert_exchange([rows_out0], [(normed0, "gather")], 3, "spread_0")
    normed_all0 = normed_all0.reshape(4 * SEQ, WIDTH)
    weights0 = of_block(0)
    sboth0, shid0, shared_part0 = moe_shared(0, normed_all0)
    both0, hid0, answer0 = moe_experts(weights0, rows_in0)
    back0, shared_got0 = expert_exchange([answer0], [(shared_part0, "swap")], 4, "collect_0")
    out0 = moe_join(hidden0, gates_wide0, back0, shared_got0)

    u1 = out0.astype(single)
    n1 = rms_scale(u1, gains[1, 0]).astype(brain)
    (n1_half,) = exchange([(shuffle(n1, mixing), "gather")], HALF, 5, "half_n1")
    n1_half = n1_half.reshape(4 * SEQ, WIDTH)
    seg_half = lax.dynamic_index_in_dim(seg_all.reshape(4, 2, SEQ), zl, 1, keepdims=False)
    qkv = dot(n1_half, w_qkv).astype(brain).astype(single).reshape(4, SEQ, QKV_COLS)
    queries = qkv[..., :384].reshape(4, SEQ, 3, HEAD_SIZE)
    keys, values = qkv[..., 384:512], qkv[..., 512:]
    probs, score_pull = jax.vjp(lambda q, k: attend_scores(q, k, seg_half), queries, keys)
    heads, mix_pull = jax.vjp(attend_mix, probs.astype(brain).astype(single), values)
    heads = heads.astype(brain).reshape(4 * SEQ, 384)
    part1 = dot(heads, w_attn).astype(brain).reshape(4, SEQ, WIDTH)
    (part1_got,) = exchange([(part1, "swap")], HALF, 6, "half_mixed")
    mixed1 = jnp.sum(part1_got.astype(single), axis=0)
    hidden1 = u1 + mixed1

    normed1, gates1, gates_wide1, rows_out1 = moe_open(1, hidden1)
    rows_in1, d_answer1, normed_all1, cot_all = expert_exchange(
        [rows_out1, back_open(cot, gates_wide1)],
        [(normed1, "gather"), (cot, "gather")],
        7,
        "spread_1",
    )
    normed_all1 = normed_all1.reshape(4 * SEQ, WIDTH)
    cot_all = cot_all.reshape(4 * SEQ, WIDTH)
    weights1 = of_block(1)
    sboth1, shid1, shared_part1 = moe_shared(1, normed_all1)
    d_sin1, d_sout1, d_shared1 = back_shared(1, cot_all, normed_all1, sboth1, shid1)
    both1, hid1, answer1 = moe_experts(weights1, rows_in1)
    d_both1, d_rows1 = back_experts(weights1, d_answer1, both1)
    back1, returned1, shared_got1, d_shared_got1 = expert_exchange(
        [answer1, d_rows1], [(shared_part1, "swap"), (d_shared1, "swap")], 8, "collect_1"
    )
    out1 = moe_join(hidden1, gates_wide1, back1, shared_got1)

    d_hid1, d_gain11, d_router1 = back_join(
        1, cot, hidden1, normed1, gates1, back1, returned1, d_shared_got1
    )
    (d_mixed1,) = exchange([(d_hid1.astype(brain), "gather")], HALF, 11, "half_dmixed")
    d_mixed1 = d_mixed1.reshape(4 * SEQ, WIDTH)
    d_heads = dot_t(d_mixed1, w_attn).reshape(4, SEQ, 3, HEAD_SIZE)
    d_attn = t_dot(heads, d_mixed1)
    d_probs, d_values = mix_pull(d_heads)
    d_queries, d_keys = score_pull(d_probs)
    d_qkv = jnp.concatenate([d_queries.reshape(4, SEQ, 384), d_keys, d_values], axis=2)
    d_qkv = d_qkv.astype(brain).reshape(4 * SEQ, QKV_COLS)
    d_w_qkv = t_dot(n1_half, d_qkv)
    d_n1_part = dot_t(d_qkv, w_qkv).astype(brain).reshape(4, SEQ, WIDTH)
    grads_wide = jnp.concatenate(
        [d_w_qkv.astype(brain).reshape(16, 96, QKV_COLS), shared_in_parts(d_sin1)], axis=2
    )
    attn_part = d_attn.astype(brain).reshape(2, 16, 12, WIDTH).transpose(1, 0, 2, 3)
    grads_tall = jnp.concatenate(
        [attn_part.reshape(16, 24, WIDTH), d_sout1.astype(brain).reshape(16, 16, WIDTH)], axis=1
    )
    grads_tall = jnp.pad(grads_tall.reshape(16, 40 * WIDTH), ((0, 0), (0, 54 * IN_COLS - 40 * WIDTH)))
    grads_later = jnp.concatenate([grads_wide, grads_tall.reshape(16, 54, IN_COLS)], axis=1)
    d_n1_part, grads_later = lax.optimization_barrier((d_n1_part, grads_later))
    grads_later = lax.psum_scatter(grads_later, RANK, scatter_dimension=0, tiled=True)[0]
    (d_n1_got,) = exchange([(d_n1_part, "swap")], HALF, 12, "half_dn1")
    d_n1 = unshuffle(jnp.sum(d_n1_got.astype(single), axis=0), mixing)
    d_u1, d_gain10 = jax.vjp(rms_scale, u1, gains[1, 0])[1](d_n1)
    d_u1 = (d_u1 + d_hid1).astype(brain)

    d_answer0, d_out0_all = expert_exchange(
        [back_open(d_u1, gates_wide0)], [(d_u1, "gather")], 13, "spread_back_0"
    )
    d_out0_all = d_out0_all.reshape(4 * SEQ, WIDTH)
    d_sin0, d_sout0, d_shared0 = back_shared(0, d_out0_all, normed_all0, sboth0, shid0)
    d_both0, d_rows0 = back_experts(weights0, d_answer0, both0)
    expert0 = (rows_in0, d_both0, hid0, d_answer0)
    expert1 = (rows_in1, d_both1, hid1, d_answer1)
    give_rows, give_both, give_hid, give_answer = (
        jnp.where(first_phase, b, a) for a, b in zip(expert0, expert1)
    )
    give_first = t_dot(give_rows, give_both).astype(brain)
    give_second = t_dot(give_hid, give_answer).astype(brain)
    d_rows0, give_first, give_second = lax.optimization_barrier((d_rows0, give_first, give_second))
    far_first = lax.ppermute(give_first, "phase", both_ways)
    far_second = lax.ppermute(give_second, "phase", both_ways)
    returned0, d_shared_got0 = expert_exchange(
        [d_rows0], [(d_shared0, "swap")], 14, "collect_back_0"
    )
    d_hid0, d_gain01, d_router0 = back_join(
        0, d_u1, hidden0, normed0, gates0, back0, returned0, d_shared_got0
    )
    d_mixed0 = d_hid0.astype(brain)
    along = jnp.sum(d_mixed0.astype(single) * mixed0, axis=1)
    scalars = jnp.stack([inverse, inverse * inverse * along / DI])
    d_mixed0, scalars_all = exchange(
        [(d_mixed0, "gather"), (pad_to(scalars, 8, 128), "gather")], TEAM, 15, "team_dmixed"
    )
    d_mixed0 = d_mixed0.reshape(PARTS * SEQ, WIDTH)
    d_yn = dot_t(d_mixed0, w_out).reshape(PARTS, SEQ, INNER)
    d_zx, yn, core_sums = by_sequence(
        mamba_backward_kernel,
        core_inputs + [d_yn, scalars_all],
        (3, 4),
        [
            jax.ShapeDtypeStruct((PARTS, SEQ, IN_COLS), brain),
            jax.ShapeDtypeStruct((PARTS, SEQ, INNER), brain),
        ],
        [jax.ShapeDtypeStruct((16, INNER + 2 * N), single)],
        "mamba_backward",
    )
    d_w_out = t_dot(yn.reshape(PARTS * SEQ, INNER), d_mixed0)
    d_zx = d_zx.reshape(PARTS * SEQ, IN_COLS)
    d_norm_gain = core_sums[6, :INNER]
    d_skip = jnp.sum(core_sums[5, :INNER].reshape(HEADS_HERE, P_SIZE), axis=1)
    d_step, d_decay = core_sums[7, :HEADS_HERE], core_sums[8, :HEADS_HERE]
    d_w_in = t_dot(n1_all, d_zx)
    d_n1_part0 = dot_t(d_zx, w_in).astype(brain).reshape(PARTS, SEQ, WIDTH)
    d_n1_part0, grads_later = lax.optimization_barrier((d_n1_part0, grads_later))
    (d_n1_got0,) = exchange([(d_n1_part0, "swap")], TEAM, 16, "team_dn1")
    d_n1_0 = unshuffle(jnp.sum(d_n1_got0.astype(single), axis=0), mixing)
    d_u0, d_gain00 = jax.vjp(rms_scale, u0, gains[0, 0])[1](d_n1_0)
    d_u0 = d_u0 + d_hid0

    def keep_and_give(block0, block1):
        return jnp.where(first_phase, block0, block1), jnp.where(first_phase, block1, block0)

    def by_block(kept, got):
        return jnp.where(first_phase, jnp.stack([kept, got]), jnp.stack([got, kept]))[None]

    keep_out, give_out = keep_and_give(out0, out1)
    keep_grad, give_grad = keep_and_give(d_u0, d_u1.astype(single))

    qkv_part = grads_later[:96, :QKV_COLS].reshape(PARTS, 12, QKV_COLS)
    sin_part1 = grads_later[:96, QKV_COLS:].reshape(4, 24, 512)
    grads_tall = grads_later[96:].reshape(54 * IN_COLS)[: 40 * WIDTH].reshape(40, WIDTH)
    attn_part, sout_part1 = grads_tall[:24].reshape(2, 12, WIDTH), grads_tall[24:]

    conv_grads = core_sums[: KW + 1]
    conv_all = jnp.concatenate(
        [
            lax.dynamic_update_slice_in_dim(
                jnp.zeros((KW + 1, DI), single), conv_grads[:, :INNER], team * INNER, 1
            ),
            conv_grads[:, INNER:],
        ],
        axis=1,
    )
    conv_all = conv_all.reshape(5, 8, 16, 26).transpose(2, 1, 0, 3).reshape(16, 8, 130)
    head_all = lax.dynamic_update_slice_in_dim(
        jnp.zeros((3, H), single), jnp.stack([d_step, d_decay, d_skip]), team * HEADS_HERE, 1
    )
    head_all = jnp.broadcast_to(head_all.reshape(1, 1, 3 * H), (16, 8, 3 * H))
    gain_all = lax.dynamic_update_slice_in_dim(
        jnp.zeros((16, 8, 24), single), d_norm_gain.reshape(16, 1, 24), team, 1
    )
    d_gains = jnp.stack([jnp.stack([d_gain00, d_gain01]), jnp.stack([d_gain10, d_gain11])])
    d_gains = d_gains.reshape(2, 2, 4, 16, 24).transpose(3, 0, 2, 1, 4).reshape(16, 8, 48)
    d_router = jnp.stack([d_router0, d_router1]).reshape(2, 4, 16, 24 * EXPERTS)
    d_router = d_router.transpose(2, 0, 1, 3).reshape(16, 8, 24 * EXPERTS)
    small_grads = jnp.concatenate([d_router, conv_all, gain_all, d_gains, head_all], axis=2)
    small_grads = jnp.pad(small_grads, ((0, 0), (0, 0), (0, 2048 - small_grads.shape[2])))
    small_grads = small_grads.astype(brain).reshape(16, 128, 128)
    d_outs = jnp.concatenate(
        [
            d_w_out.astype(brain).reshape(16, 24, WIDTH),
            d_sout0.astype(brain).reshape(16, 16, WIDTH),
            jnp.zeros((16, 8, WIDTH), brain),
        ],
        axis=1,
    )
    main_part, outs_part, sin_part0, small_part, got_out, got_grad = rank_sum(
        [
            d_w_in.astype(brain).reshape(16, 96, IN_COLS),
            d_outs,
            shared_in_parts(d_sin0),
            small_grads,
        ],
        [give_out, give_grad],
        17,
        "rank_grads",
    )
    phase_outputs = by_block(keep_out, got_out)
    input_grads = by_block(keep_grad, got_grad)
    main_part = main_part.reshape(PARTS, 12, IN_COLS)
    out_proj_grad, sout_part0 = outs_part[:24], outs_part[24:40]
    sin_part0 = sin_part0.reshape(4, 24, 512)

    rows_kept, d_both_kept, hid_kept, d_answer_kept = (
        jnp.where(first_phase, a, b) for a, b in zip(expert0, expert1)
    )
    far_first, far_second = after((far_first, far_second), main_part)
    experts_in_grad = t_dot(rows_kept, d_both_kept) + far_first.astype(single)
    experts_out_grad = t_dot(hid_kept, d_answer_kept) + far_second.astype(single)

    main_end, qkv_end, sin_end, sout_end, attn_end, small_end = exchange(
        [
            (pad_rows(main_part, 16), "swap"),
            (pad_rows(qkv_part, 16), "swap"),
            (pad_rows(jnp.concatenate([sin_part0, sin_part1], axis=0), 32), "swap"),
            (jnp.stack([sout_part0, sout_part1]), "phase"),
            (pad_rows(attn_part, 16), "zl"),
            (small_part.reshape(PARTS, 16, 128), "swap"),
        ],
        TEAM,
        18,
        "team_end",
    )
    rows_end = main_end[:, :12].astype(single)

    def side_by_side(value):
        return value.transpose(1, 0, 2).reshape(value.shape[1], -1)

    in_proj_grad = jnp.concatenate(
        [
            side_by_side(rows_end[:, :, :INNER]),
            side_by_side(rows_end[:, :, INNER : 2 * INNER]),
            jnp.sum(rows_end[:, :, 2 * INNER : 2 * INNER + 2 * N], axis=0),
            side_by_side(
                rows_end[:, :, 2 * INNER + 2 * N : 2 * INNER + 2 * N + HEADS_HERE]
            ),
        ],
        axis=1,
    )
    small_end = jnp.sum(small_end.astype(single), axis=0).reshape(2048)
    router_grad = small_end[: 24 * EXPERTS].reshape(1, 24, EXPERTS)
    at = 24 * EXPERTS
    conv_end = small_end[at : at + 130].reshape(5, 26)
    at += 130
    norm_gain_grad = small_end[at : at + 24]
    at += 24
    norm_gains_grad = small_end[at : at + 48].reshape(1, 2, 24)
    at += 48
    heads_end = small_end[at : at + 3 * H].reshape(3, H)
    qkv_end = qkv_end[:, :12].astype(single).reshape(4, 2, 12, QKV_COLS)
    qkv_end = jnp.sum(qkv_end, axis=1)
    query_grad = side_by_side(qkv_end[:, :, :384])
    kv_grad = qkv_end[:, :, 384:].reshape(4, 12, 2, 128).transpose(1, 2, 0, 3).reshape(12, 1024)
    sin_end = jnp.sum(sin_end[:, :24].astype(single).reshape(2, 4, 24, 2, 256), axis=0)
    shared_in_grad = sin_end.transpose(1, 2, 0, 3).reshape(1, 24, 2048)
    shared_out_grad = jnp.sum(sout_end.astype(single), axis=0)[None]
    attn_out_grad = jnp.sum(attn_end[:, :12].astype(single), axis=0)

    return (
        phase_outputs,
        input_grads,
        in_proj_grad,
        conv_end[:KW],
        conv_end[KW],
        heads_end[0],
        heads_end[1],
        heads_end[2],
        norm_gain_grad,
        out_proj_grad.astype(single),
        query_grad,
        kv_grad,
        attn_out_grad,
        norm_gains_grad,
        router_grad,
        shared_in_grad,
        shared_out_grad,
        experts_in_grad[None, None],
        experts_out_grad[None, None],
    )


def solution(mesh):
    fine = Mesh(mesh.devices.reshape(tuple(SIZES.values())), ALL)
    in_specs = (
        P(None, DP, None),
        P(None, DP, None),
        P(None, DP, None),
        P(None, DP, None),
        P(ALL, None),
        P(None, ALL),
        P(ALL),
        P(),
        P(),
        P(),
        P(ALL),
        P(ALL, None),
        P(ALL, None),
        P(ALL, None),
        P(ALL, None),
        P("phase", None, DP),
        P("phase", DP, None),
        P("phase", DP, None),
        P("phase", DP, None),
        P("phase", DP, None, None),
        P("phase", DP, None, None),
    )
    out_specs = (
        P("phase", None, DP, None),
        P("phase", None, DP, None),
        P(ALL, None),
        P(None, ALL),
        P(ALL),
        P(),
        P(),
        P(),
        P(ALL),
        P(ALL, None),
        P(ALL, None),
        P(ALL, None),
        P(ALL, None),
        P("phase", None, DP),
        P("phase", DP, None),
        P("phase", DP, None),
        P("phase", DP, None),
        P("phase", DP, None, None),
        P("phase", DP, None, None),
    )
    return jax.shard_map(
        per_device, mesh=fine, in_specs=in_specs, out_specs=out_specs, check_vma=False
    )
```

profile of v0, /device:TPU:0, one launch (start us, length us, event | category | flops | bytes accessed | tf_op | source)
XLA Modules:
  0.0 925.0 jit_solution(7299283052980820627)
XLA Ops:
  11.0 14.8 %team_start.1 = (bf16[8,16,1152]{2,1,0:T(8,128)(2,1)S(1)}, bf16[8,32,512]{2,1,0:T(8,128)(2,1)S(1)}, bf16[2,16,1536]{2,1,0:T(8,128)(2,1)S(1)}, bf16[8,16,128]{2,1,0:T(8,128)(2,1)S(1)}, s32[8,8,128]{2,1,0:T(8,128)S(1)}) custom-call(bf16[8,16,1152]{2,1,0:T(8,128)(2,1)S(1)} %pad.113.refs_0_, bf16[8,32,512]{2,1,0:T(8,128)(2,1)S(1)} %fusion.143.refs_1_, ...), custom_call_target="tpu_custom_call" | custom-call | flops 20000000000 | bytes 1441792 | tf_op jit(solution)/shard_map/team_start/pallas_call | solution.py:151
  28.1 1.9 fusion.32.refs_5_
  30.8 43.8 %rank_weights.1 = (bf16[16,96,1152]{2,1,0:T(8,128)(2,1)}, bf16[16,128,128]{2,1,0:T(8,128)(2,1)S(1)}, bf16[16,32,1536]{2,1,0:T(8,128)(2,1)S(1)}, bf16[16,96,512]{...) custom-call(bf16[96,1152]{1,0:T(8,128)(2,1)S(1)} %copy-done.35, ...), custom_call_target="tpu_custom_call" | custom-call | flops 40000000000 | bytes 19660800 | tf_op jit(solution)/shard_map/rank_weights/pallas_call | solution.py:151
  79.9 1.6 collective-permute-start.1
  82.2 1.7 pad_maximum_fusion.3
  88.7 1.8 copy.361
  92.8 2.4 fusion.77
  96.5 2.7 reshape.892
  101.1 2.1 fusion.260
  106.3 1.8 copy.374
  108.8 4.8 fusion.65.zx_ref
  113.7 8.1 mamba_forward.1
  124.2 2.2 convolution_convert_fusion.9
  126.4 76.0 %collective-permute-done.1 = bf16[512,1536]{1,0:T(8,128)(2,1)} collective-permute-done((bf16[512,1536]{1,0:T(8,128)(2,1)}, bf16[512,1536]{1,0:T(8,128)(2,1)}, u32[]{:S(2)}, u32[]{:S(2)}) %collective-permute-start.1) | collective-permute-done | bytes 1572896 | tf_op jit(solution)/shard_map/ppermute | solution.py:804
  202.4 22.1 %team_mixed_0.1 = (bf16[8,64,1536]{2,1,0:T(8,128)(2,1)S(1)}, f32[8,8,128]{2,1,0:T(8,128)S(1)}) custom-call(bf16[8,64,1536]{2,1,0:T(8,128)(2,1)S(1)} %bitcast.530, f32[8,8,128]{2,1,0:T(8,128)S(1)} %get-tuple-element.90.refs_1_), custom_call_target="tpu_custom_call" | custom-call | flops 20000000000 | bytes 3211264 | tf_op jit(solution)/shard_map/team_mixed_0/pallas_call | solution.py:151
  226.6 36.3 %spread_0.1 = (bf16[64,8,1536]{2,1,0:T(8,128)(2,1)S(1)}, bf16[4,64,1536]{2,1,0:T(8,128)(2,1)S(1)}) custom-call(bf16[64,8,1536]{2,1,0:T(8,128)(2,1)S(1)} %fusion.17.refs_0_, bf16[64,1536]{1,0:T(8,128)(2,1)S(1)} %multiply_convert_fusion.3.refs_1_), custom_call_target="tpu_custom_call" | custom-call | flops 40000000000 | bytes 4718592 | tf_op jit(solution)/shard_map/spread_0/pallas_call | solution.py:151
  262.9 1.9 fusion.58
  269.5 32.1 %collect_0.1 = (bf16[64,8,1536]{2,1,0:T(8,128)(2,1)S(1)}, bf16[4,64,1536]{2,1,0:T(8,128)(2,1)S(1)}) custom-call(bf16[64,8,1536]{2,1,0:T(8,128)(2,1)S(1)} %fusion.20.refs_0_, bf16[4,64,1536]{2,1,0:T(8,128)(2,1)S(1)} %bitcast.542), custom_call_target="tpu_custom_call" | custom-call | flops 40000000000 | bytes 4718592 | tf_op jit(solution)/shard_map/collect_0/pallas_call | solution.py:151
  304.3 1.9 fusion.33.refs_0_
  306.3 17.6 %half_n1.1 = bf16[4,64,1536]{2,1,0:T(8,128)(2,1)S(1)} custom-call(bf16[64,1536]{1,0:T(8,128)(2,1)S(1)} %fusion.33.refs_0_), custom_call_target="tpu_custom_call" | custom-call | flops 20000000000 | bytes 1572864 | tf_op jit(solution)/shard_map/half_n1/pallas_call | solution.py:151
  323.9 1.6 slice.399
  330.1 1.7 slice.395
  331.9 2.3 slice.404
  337.4 12.7 %half_mixed.1 = bf16[4,64,1536]{2,1,0:T(8,128)(2,1)S(1)} custom-call(bf16[4,64,1536]{2,1,0:T(8,128)(2,1)S(1)} %bitcast.533), custom_call_target="tpu_custom_call" | custom-call | flops 20000000000 | bytes 1572864 | tf_op jit(solution)/shard_map/half_mixed/pallas_call | solution.py:151
  351.0 1.8 fusion.18.refs_0_
  355.0 1.8 fusion.23.refs_1_
  356.8 59.9 %spread_1.1 = (bf16[64,8,1536]{2,1,0:T(8,128)(2,1)S(1)}, bf16[64,8,1536]{2,1,0:T(8,128)(2,1)S(1)}, bf16[4,64,1536]{2,1,0:T(8,128)(2,1)S(1)}, bf16[4,64,1536]{2,1,0:T(8,128)(2,1)S(1)}) custom-call(bf16[64,8,1536]{2,1,0:T(8,128)(2,1)} %fusion.18.refs_0_, bf16[64,8,1536]{2,1,0:T(8,128)(2,1)} %fusion.23.refs_1_, ...), custom_call_target="tpu_custom_call" | custom-call | flops 80000000000 | bytes 9437184 | tf_op jit(solution)/shard_map/spread_1/pallas_call | solution.py:151
  419.6 3.8 fusion.48
  423.4 2.8 fusion.170
  426.3 4.5 fusion.21.refs_0_
  430.8 4.9 fusion.19.refs_1_
  435.7 60.3 %collect_1.1 = (bf16[64,8,1536]{2,1,0:T(8,128)(2,1)S(1)}, bf16[64,8,1536]{2,1,0:T(8,128)(2,1)}, bf16[4,64,1536]{2,1,0:T(8,128)(2,1)S(1)}, bf16[4,64,1536]{2,1,0:T(8,128)(2,1)S(1)}) custom-call(bf16[64,8,1536]{2,1,0:T(8,128)(2,1)} %fusion.21.refs_0_, bf16[64,8,1536]{2,1,0:T(8,128)(2,1)} %fusion.19.refs_1_, bf16[4,64,1536]{2,1,0:T(8,128)(2,1)S(1)} %bitcast.540, ...), custom_call_target="tpu_custom_call" | custom-call | flops 80000000000 | bytes 9437184 | tf_op jit(solution)/shard_map/collect_1/pallas_call | solution.py:151
  499.9 13.0 %half_dmixed.1 = bf16[4,64,1536]{2,1,0:T(8,128)(2,1)S(1)} custom-call(bf16[64,1536]{1,0:T(8,128)(2,1)S(1)} %fusion.254.refs_0_), custom_call_target="tpu_custom_call" | custom-call | flops 20000000000 | bytes 1572864 | tf_op jit(solution)/shard_map/half_dmixed/pallas_call | solution.py:151
  517.0 1.8 convolution_convert_fusion.7
  523.2 2.1 reshape.933
  528.2 3.4 reshape.937
  536.0 3.7 pad_maximum_fusion
  539.6 13.6 %half_dn1.1 = bf16[4,64,1536]{2,1,0:T(8,128)(2,1)S(1)} custom-call(bf16[4,64,1536]{2,1,0:T(8,128)(2,1)S(1)} %bitcast.556), custom_call_target="tpu_custom_call" | custom-call | flops 20000000000 | bytes 1572864 | tf_op jit(solution)/shard_map/half_dn1/pallas_call | solution.py:151
  553.9 2.0 fusion.1
  558.6 34.0 %spread_back_0.1 = (bf16[64,8,1536]{2,1,0:T(8,128)(2,1)S(1)}, bf16[4,64,1536]{2,1,0:T(8,128)(2,1)S(1)}) custom-call(bf16[64,8,1536]{2,1,0:T(8,128)(2,1)S(1)} %fusion.22.refs_0_, bf16[64,1536]{1,0:T(8,128)(2,1)S(1)} %fusion.104.refs_1_), custom_call_target="tpu_custom_call" | custom-call | flops 40000000000 | bytes 4718592 | tf_op jit(solution)/shard_map/spread_back_0/pallas_call | solution.py:151
  592.7 2.2 convolution_convert_fusion.2
  599.1 3.5 convolution_convert_fusion
  602.7 1.8 convolution_convert_fusion.6
  606.7 31.4 %collect_back_0.1 = (bf16[64,8,1536]{2,1,0:T(8,128)(2,1)S(1)}, bf16[4,64,1536]{2,1,0:T(8,128)(2,1)S(1)}) custom-call(bf16[64,8,1536]{2,1,0:T(8,128)(2,1)S(1)} %bitcast.554, bf16[4,64,1536]{2,1,0:T(8,128)(2,1)S(1)} %bitcast.543), custom_call_target="tpu_custom_call" | custom-call | flops 40000000000 | bytes 4718592 | tf_op jit(solution)/shard_map/collect_back_0/pallas_call | solution.py:151
  641.8 25.0 %team_dmixed.1 = (bf16[8,64,1536]{2,1,0:T(8,128)(2,1)S(1)}, f32[8,8,128]{2,1,0:T(8,128)S(1)}) custom-call(bf16[64,1536]{1,0:T(8,128)(2,1)S(1)} %get-tuple-element.158.refs_0_, f32[8,128]{1,0:T(8,128)S(1)} %select_maximum_fusion.refs_1_), custom_call_target="tpu_custom_call" | custom-call | flops 20000000000 | bytes 3211264 | tf_op jit(solution)/shard_map/team_dmixed/pallas_call | solution.py:151
  669.1 14.0 %mamba_backward.1 = (bf16[8,64,1152]{2,1,0:T(8,128)(2,1)S(1)}, bf16[8,64,384]{2,1,0:T(8,128)(2,1)S(1)}, f32[16,640]{1,0:T(8,128)S(1)}) custom-call(f32[8,64,1152]{2,1,0:T(8,128)S(1)} %copy-done.7, f32[8,64,64]{2,1,0:T(8,128)S(1)} %and_convert_fusion.masks_ref, f32[8,64,128]{2,1,0:T(8,128)S(1)} %copy-done.13, f32[8,640]{1,0:T(8,128)S(1)} %maximum_maximum_fusion.1.taps_ref, ...), custom_call_target="tpu_custom_call" | custom-call | tf_op jit(solution)/shard_map/mamba_backward/pallas_call | solution.py:689
  695.5 1.6 convolution_convert_fusion.13
  701.4 2.7 fusion.37
  705.7 4.5 fusion.50
  710.2 2.0 maximum_maximum_fusion.refs_1_
  712.3 2.2 convolution_convert_fusion.1
  714.5 4.1 fusion.5
  718.6 12.9 %reduce-scatter.4.cloned.1.call-done = bf16[1,150,1152]{2,1,0:T(8,128)(2,1)} async-done(((bf16[16,150,1152]{2,1,0:T(8,128)(2,1)}), bf16[1,150,1152]{2,1,0:T(8,128)(2,1)}) %reduce-scatter.4.cloned.1.call-update) | async-done | bytes 345616
  731.6 1.6 slice.354
  733.1 1.5 slice.355
  734.7 1.6 slice.357
  736.2 1.5 slice.359
  737.8 77.4 %team_dn1.1 = bf16[8,64,1536]{2,1,0:T(8,128)(2,1)S(1)} custom-call(bf16[8,64,1536]{2,1,0:T(8,128)(2,1)S(1)} %bitcast.553), custom_call_target="tpu_custom_call" | custom-call | flops 20000000000 | bytes 3145728 | tf_op jit(solution)/shard_map/team_dn1/pallas_call | solution.py:151
  816.0 2.0 fusion
  822.9 2.4 fusion.105
  825.4 47.6 %rank_grads.1 = (bf16[96,1152]{1,0:T(8,128)(2,1)S(1)}, bf16[48,1536]{1,0:T(8,128)(2,1)S(1)}, bf16[96,512]{1,0:T(8,128)(2,1)S(1)}, bf16[128,128]{1,0:T(8,128)(2,1...) custom-call(bf16[8,2,96,1152]{3,2,1,0:T(8,128)(2,1)} %bitcast.651, bf16[8,2,48,1536]{3,2,1,0:T(8,128)(2,1)S(1)} %copy-done.14, ...), custom_call_target="tpu_custom_call" | custom-call | flops 44999999488 | bytes 2179072 | tf_op jit(solution)/shard_map/rank_grads/pallas_call | solution.py:151
  875.3 19.2 %team_end.1 = (bf16[8,16,1152]{2,1,0:T(8,128)(2,1)S(1)}, bf16[8,16,640]{2,1,0:T(8,128)(2,1)S(1)}, bf16[8,32,512]{2,1,0:T(8,128)(2,1)S(1)}, bf16[2,16,1536]{2,1,0...) custom-call(bf16[8,16,1152]{2,1,0:T(8,128)(2,1)S(1)} %pad.139.refs_0_, ...), custom_call_target="tpu_custom_call" | custom-call | flops 20000000000 | bytes 1900544 | tf_op jit(solution)/shard_map/team_end/pallas_call | solution.py:151
  905.5 8.2 add_bitcast_fusion
  913.7 3.5 add_bitcast_fusion.1
  (800 shorter events, 122.8 us)
Async XLA Ops:
  7.2 89.2 %copy-start = (s32[2,64,6]{1,0,2:T(2,128)S(1)}, s32[2,64,6]{1,0,2:T(2,128)}, u32[]{:S(2)}) copy-start(s32[2,64,6]{1,0,2:T(2,128)} %param.24) | copy-start | bytes 9220
  7.3 316.7 %all-gather.7.cloned.1.call-start = ((), (), s32[]{:S(2)}) async-start(), calls=%async_computation.2 | async-start | bytes 2088960 | tf_op jit(solution)/shard_map/all_gather | solution.py:806
  9.0 19.1 %copy-start.180 = (s32[1536]{0:T(1024)}, s32[1536]{0:T(1024)S(1)}, u32[]{:S(2)}) copy-start(s32[1536]{0:T(1024)S(1)} %fusion.200) | copy-start | bytes 18436
  10.9 15.6 %copy-start.156 = (bf16[24,1536]{1,0:T(8,128)(2,1)S(1)}, bf16[24,1536]{1,0:T(8,128)(2,1)}, u32[]{:S(2)}) copy-start(bf16[24,1536]{1,0:T(8,128)(2,1)} %param.32) | copy-start | bytes 221188
  10.9 16.9 %copy-start.168 = (bf16[12,1024]{1,0:T(8,128)(2,1)S(1)}, bf16[12,1024]{1,0:T(8,128)(2,1)}, u32[]{:S(2)}) copy-start(bf16[12,1024]{1,0:T(8,128)(2,1)} %param.34) | copy-start | bytes 73732
  10.9 16.9 %copy-start.162 = (bf16[12,1536]{1,0:T(8,128)(2,1)S(1)}, bf16[12,1536]{1,0:T(8,128)(2,1)}, u32[]{:S(2)}) copy-start(bf16[12,1536]{1,0:T(8,128)(2,1)} %param.33) | copy-start | bytes 110596
  79.4 250.8 %all-gather.5.cloned.1.call-start = ((), (), s32[]{:S(2)}) async-start(), calls=%async_computation.1 | async-start | bytes 3760128 | tf_op jit(solution)/shard_map/all_gather | solution.py:805
  79.4 123.0 %collective-permute-start = (bf16[1536,1024]{1,0:T(8,128)(2,1)}, bf16[1536,1024]{1,0:T(8,128)(2,1)}, u32[]{:S(2)}, u32[]{:S(2)}) collective-permute-start(bf16[1536,1024]{1,0:T(8,128)(2,1)} %bitcast.647), channel_id=1, source_target_pairs={{0,64},{64,0},{1,65},{65,1},{2,66},{66,2},{3,67},{67,3},{4,68},{68... | collective-permute-start | bytes 9437192 | tf_op jit(solution)/shard_map/ppermute | solution.py:803
  79.9 122.6 %collective-permute-start.1 = (bf16[512,1536]{1,0:T(8,128)(2,1)}, bf16[512,1536]{1,0:T(8,128)(2,1)}, u32[]{:S(2)}, u32[]{:S(2)}) collective-permute-start(bf16[512,1536]{1,0:T(8,128)(2,1)} %bitcast.648), channel_id=1, source_target_pairs={{0,64},{64,0},{1,65},{65,1},{2,66},{66,2},{3,67},{67,3},{4,68},{68... | collective-permute-start | bytes 4718600 | tf_op jit(solution)/shard_map/ppermute | solution.py:804
  83.9 647.7 %reduce-scatter.4.cloned.1.call-start = ((), (), s32[]{:S(2)}) async-start(), calls=%async_computation.3 | async-start | bytes 5953536
  92.7 175.0 %copy-start.137 = (f32[1536]{0:T(1024)}, f32[1536]{0:T(1024)S(1)}, u32[]{:S(2)}) copy-start(f32[1536]{0:T(1024)S(1)} %get-tuple-element.151) | copy-start | bytes 18436
  92.7 211.6 %copy-start.154 = (f32[1536]{0:T(1024)}, f32[1536]{0:T(1024)S(1)}, u32[]{:S(2)}) copy-start(f32[1536]{0:T(1024)S(1)} %get-tuple-element.150) | copy-start | bytes 18436
  95.3 4.8 slice-start
  96.5 8.8 copy-start.170
  103.2 5.6 copy-start.178
  105.3 160.9 %copy-start.50 = (bf16[16,4,24,512]{3,2,0,1:T(8,128)(2,1)}, bf16[16,4,24,512]{3,2,0,1:T(8,128)(2,1)S(1)}, u32[]{:S(2)}) copy-start(bf16[16,4,24,512]{3,2,0,1:T(8,128)(2,1)S(1)} %copy.367) | copy-start | bytes 4718596
  105.4 247.7 %copy-start.122 = (pred[64,64]{0,1:T(32,128)(4,1)}, pred[64,64]{0,1:T(32,128)(4,1)S(1)}, u32[]{:S(2)}) copy-start(pred[64,64]{0,1:T(32,128)(4,1)S(1)} %copy.366) | copy-start | bytes 12292
  106.2 161.5 %copy-start.69 = (bf16[1,4,16,24,64]{4,3,2,1,0:T(8,128)(2,1)}, bf16[1,4,16,24,64]{4,3,2,1,0:T(8,128)(2,1)S(1)}, u32[]{:S(2)}) copy-start(bf16[1,4,16,24,64]{4,3,2,1,0:T(8,128)(2,1)S(1)} %copy.364) | copy-start | bytes 589828
  106.3 229.1 %copy-start.139 = (pred[4,64,64]{1,2,0:T(8,128)(4,1)}, pred[4,64,64]{1,2,0:T(8,128)(4,1)S(1)}, u32[]{:S(2)}) copy-start(pred[4,64,64]{1,2,0:T(8,128)(4,1)S(1)} %copy.368) | copy-start | bytes 49156
  113.7 9.5 %copy-start.171 = (pred[64,64]{1,0:T(8,128)(4,1)S(1)}, pred[64,64]{1,0:T(8,128)(4,1)}, u32[]{:S(2)}) copy-start(pred[64,64]{1,0:T(8,128)(4,1)} %copy-done.170) | copy-start | bytes 12292
  113.7 9.8 %copy-start.118 = (bf16[2,64,1536]{2,1,0:T(8,128)(2,1)S(1)}, bf16[2,64,1536]{2,1,0:T(8,128)(2,1)}, u32[]{:S(2)}) copy-start(bf16[2,64,1536]{2,1,0:T(8,128)(2,1)} %param.22) | copy-start | bytes 1179652
  123.2 229.9 %copy-start.208 = (s32[512]{0:T(512)}, s32[512]{0:T(512)S(1)}, u32[]{:S(2)}) copy-start(s32[512]{0:T(512)S(1)} %get-tuple-element.218) | copy-start | bytes 6148
  123.5 230.8 %copy-start.79 = (pred[64,512]{1,0:T(32,128)(4,1)}, pred[64,512]{1,0:T(32,128)(4,1)S(1)}, u32[]{:S(2)}) copy-start(pred[64,512]{1,0:T(32,128)(4,1)S(1)} %convolution_compare_fusion) | copy-start | bytes 98308
  224.8 42.9 %copy-start.61 = (f32[64,1536]{1,0:T(8,128)}, f32[64,1536]{1,0:T(8,128)S(1)}, u32[]{:S(2)}) copy-start(f32[64,1536]{1,0:T(8,128)S(1)} %convert_reduce_fusion.1) | copy-start | bytes 1179652
  225.5 42.2 %copy-start.192 = (f32[64]{0:T(128)}, f32[64]{0:T(128)S(1)}, u32[]{:S(2)}) copy-start(f32[64]{0:T(128)S(1)} %get-tuple-element.195) | copy-start | bytes 772
  225.7 37.1 %copy-start.221 = (f32[64]{0:T(128)}, f32[64]{0:T(128)S(1)}, u32[]{:S(2)}) copy-start(f32[64]{0:T(128)S(1)} %get-tuple-element.163) | copy-start | bytes 772
  225.8 77.4 %copy-start.52 = (f32[64,1536]{1,0:T(8,128)}, f32[64,1536]{1,0:T(8,128)S(1)}, u32[]{:S(2)}) copy-start(f32[64,1536]{1,0:T(8,128)S(1)} %get-tuple-element.164) | copy-start | bytes 1179652
  225.8 78.0 %copy-start.218 = (f32[64]{0:T(128)}, f32[64]{0:T(128)S(1)}, u32[]{:S(2)}) copy-start(f32[64]{0:T(128)S(1)} %get-tuple-element.181) | copy-start | bytes 772
  225.8 41.9 %copy-start.175 = (f32[64]{0:T(128)}, f32[64]{0:T(128)S(1)}, u32[]{:S(2)}) copy-start(f32[64]{0:T(128)S(1)} %fusion.226) | copy-start | bytes 772
  225.9 37.0 %copy-start.15 = (bf16[64,1536]{1,0:T(8,128)(2,1)}, bf16[64,1536]{1,0:T(8,128)(2,1)S(1)}, u32[]{:S(2)}) copy-start(bf16[64,1536]{1,0:T(8,128)(2,1)S(1)} %multiply_convert_fusion.3.refs_1_) | copy-start | bytes 589828
  226.5 36.4 %copy-start.233 = (bf16[1,1,1536,1024]{3,2,1,0:T(8,128)(2,1)S(1)}, bf16[1,1,1536,1024]{3,2,1,0:T(8,128)(2,1)}, u32[]{:S(2)}) copy-start(bf16[1,1,1536,1024]{3,2,1,0:T(8,128)(2,1)} %param.40) | copy-start | bytes 9437188
  268.1 33.7 %copy-start.126 = (f32[64,64]{0,1:T(8,128)}, f32[64,64]{0,1:T(8,128)S(1)}, u32[]{:S(2)}) copy-start(f32[64,64]{0,1:T(8,128)S(1)} %get-tuple-element.197) | copy-start | bytes 49156
  268.1 33.7 %copy-start.184 = (f32[64]{0:T(128)}, f32[64]{0:T(128)S(1)}, u32[]{:S(2)}) copy-start(f32[64]{0:T(128)S(1)} %get-tuple-element.196) | copy-start | bytes 772
  268.5 33.3 %copy-start.194 = (f32[64]{0:T(128)}, f32[64]{0:T(128)S(1)}, u32[]{:S(2)}) copy-start(f32[64]{0:T(128)S(1)} %fusion.186) | copy-start | bytes 772
  303.7 46.6 %copy-start.63 = (bf16[64,1536]{1,0:T(8,128)(2,1)}, bf16[64,1536]{1,0:T(8,128)(2,1)S(1)}, u32[]{:S(2)}) copy-start(bf16[64,1536]{1,0:T(8,128)(2,1)S(1)} %get-tuple-element.199) | copy-start | bytes 589828
  323.9 10.2 %copy-start.42 = (bf16[4,64,1536]{2,1,0:T(8,128)(2,1)}, bf16[4,64,1536]{2,1,0:T(8,128)(2,1)S(1)}, u32[]{:S(2)}) copy-start(bf16[4,64,1536]{2,1,0:T(8,128)(2,1)S(1)} %half_n1.1) | copy-start | bytes 2359300
  336.8 13.4 %copy-start.90 = (bf16[4,64,3,128]{3,2,1,0:T(4,128)(2,1)}, bf16[4,64,3,128]{3,2,1,0:T(4,128)(2,1)S(1)}, u32[]{:S(2)}) copy-start(bf16[4,64,3,128]{3,2,1,0:T(4,128)(2,1)S(1)} %copy.371) | copy-start | bytes 589828
  350.9 5.8 copy-start.8
  416.6 6.8 copy-start.24
  435.7 60.6 %copy-start.80 = (pred[64,512]{1,0:T(32,128)(4,1)S(1)}, pred[64,512]{1,0:T(32,128)(4,1)}, u32[]{:S(2)}) copy-start(pred[64,512]{1,0:T(32,128)(4,1)} %copy-done.79) | copy-start | bytes 98308
  496.0 16.9 %copy-start.30 = (bf16[4,64,1536]{2,1,0:T(8,128)(2,1)}, bf16[4,64,1536]{2,1,0:T(8,128)(2,1)S(1)}, u32[]{:S(2)}) copy-start(bf16[4,64,1536]{2,1,0:T(8,128)(2,1)S(1)} %get-tuple-element.106) | copy-start | bytes 2359300
  499.7 13.2 %copy-start.73 = (f32[64,1536]{1,0:T(8,128)}, f32[64,1536]{1,0:T(8,128)S(1)}, u32[]{:S(2)}) copy-start(f32[64,1536]{1,0:T(8,128)S(1)} %get-tuple-element.208) | copy-start | bytes 1179652
  499.8 13.0 %copy-start.67 = (bf16[3,128,1536,1]{2,1,0,3:T(8,128)(2,1)S(1)}, bf16[3,128,1536,1]{2,1,0,3:T(8,128)(2,1)}, u32[]{:S(2)}) copy-start(bf16[3,128,1536,1]{2,1,0,3:T(8,128)(2,1)} %reshape.990) | copy-start | bytes 3538948
  558.6 34.0 %copy-start.25 = (bf16[64,8,1536]{2,1,0:T(8,128)(2,1)S(1)}, bf16[64,8,1536]{2,1,0:T(8,128)(2,1)}, u32[]{:S(2)}) copy-start(bf16[64,8,1536]{2,1,0:T(8,128)(2,1)} %copy-done.24) | copy-start | bytes 4718596
  558.6 34.0 %copy-start.86 = (bf16[512,512]{1,0:T(8,128)(2,1)S(1)}, bf16[512,512]{1,0:T(8,128)(2,1)}, u32[]{:S(2)}) copy-start(bf16[512,512]{1,0:T(8,128)(2,1)} %copy-done.85) | copy-start | bytes 1572868
  558.6 34.0 %copy-start.132 = (bf16[512,512]{1,0:T(8,128)(2,1)S(1)}, bf16[512,512]{1,0:T(8,128)(2,1)}, u32[]{:S(2)}) copy-start(bf16[512,512]{1,0:T(8,128)(2,1)} %copy-done.131) | copy-start | bytes 1572868
  592.6 11.9 %copy-start.34 = (bf16[4,64,1536]{2,1,0:T(8,128)(2,1)}, bf16[4,64,1536]{2,1,0:T(8,128)(2,1)S(1)}, u32[]{:S(2)}) copy-start(bf16[4,64,1536]{2,1,0:T(8,128)(2,1)S(1)} %get-tuple-element.112) | copy-start | bytes 2359300
  597.4 5.2 copy-start.110
  597.4 5.2 copy-start.112
  606.7 31.6 %copy-start.124 = (pred[64,64]{0,1:T(32,128)(4,1)S(1)}, pred[64,64]{0,1:T(32,128)(4,1)}, u32[]{:S(2)}) copy-start(pred[64,64]{0,1:T(32,128)(4,1)} %copy-done.122) | copy-start | bytes 12292
  606.7 31.6 %copy-start.127 = (f32[64,64]{0,1:T(8,128)S(1)}, f32[64,64]{0,1:T(8,128)}, u32[]{:S(2)}) copy-start(f32[64,64]{0,1:T(8,128)} %copy-done.126) | copy-start | bytes 49156
  606.7 31.6 %copy-start.185 = (f32[64]{0:T(128)S(1)}, f32[64]{0:T(128)}, u32[]{:S(2)}) copy-start(f32[64]{0:T(128)} %copy-done.184) | copy-start | bytes 772
  606.7 31.6 %copy-start.195 = (f32[64]{0:T(128)S(1)}, f32[64]{0:T(128)}, u32[]{:S(2)}) copy-start(f32[64]{0:T(128)} %copy-done.194) | copy-start | bytes 772
  606.7 31.6 %copy-start.210 = (s32[512]{0:T(512)S(1)}, s32[512]{0:T(512)}, u32[]{:S(2)}) copy-start(s32[512]{0:T(512)} %copy-done.208) | copy-start | bytes 6148
  641.8 25.1 %copy-start.66 = (bf16[16,24,1536]{2,1,0:T(8,128)(2,1)S(1)}, bf16[16,24,1536]{2,1,0:T(8,128)(2,1)}, u32[]{:S(2)}) copy-start(bf16[16,24,1536]{2,1,0:T(8,128)(2,1)} %slice.318) | copy-start | bytes 3538948
  669.1 14.1 %copy-start.11 = (bf16[4,64,1536]{2,1,0:T(8,128)(2,1)S(1)}, bf16[4,64,1536]{2,1,0:T(8,128)(2,1)}, u32[]{:S(2)}) copy-start(bf16[4,64,1536]{2,1,0:T(8,128)(2,1)} %copy-done.10) | copy-start | bytes 2359300
  669.1 14.1 %copy-start.115 = (f32[256,256]{1,0:T(8,128)S(1)}, f32[256,256]{1,0:T(8,128)}, u32[]{:S(2)}) copy-start(f32[256,256]{1,0:T(8,128)} %copy-done.114) | copy-start | bytes 786436
  669.1 14.1 %copy-start.117 = (f32[256,256]{1,0:T(8,128)S(1)}, f32[256,256]{1,0:T(8,128)}, u32[]{:S(2)}) copy-start(f32[256,256]{1,0:T(8,128)} %copy-done.116) | copy-start | bytes 786436
  686.5 8.9 copy-start.103
  688.8 8.3 copy-start.3
  692.0 211.7 %collective-permute-start.2 = (bf16[1536,1024]{1,0:T(8,128)(2,1)}, bf16[1536,1024]{1,0:T(8,128)(2,1)}, u32[]{:S(2)}, u32[]{:S(2)}) collective-permute-start(bf16[1536,1024]{1,0:T(8,128)(2,1)} %convolution_convert_fusion), channel_id=1, source_target_pairs={{0,64},{64,0},{1,65},{65,1},{2,66},{66,2},{3,67},{67,3},{4,68},{68... | collective-permute-start | bytes 9437192 | tf_op jit(solution)/shard_map/ppermute | solution.py:1033
  692.8 211.0 %collective-permute-start.3 = (bf16[512,1536]{1,0:T(8,128)(2,1)}, bf16[512,1536]{1,0:T(8,128)(2,1)}, u32[]{:S(2)}, u32[]{:S(2)}) collective-permute-start(bf16[512,1536]{1,0:T(8,128)(2,1)} %convolution_convert_fusion.2), channel_id=1, source_target_pairs={{0,64},{64,0},{1,65},{65,1},{2,66},{66,2},{3,67},{67,3},{4,68},{68... | collective-permute-start | bytes 4718600 | tf_op jit(solution)/shard_map/ppermute | solution.py:1034
  705.7 6.6 copy-start.243
  905.5 8.2 copy-start.58
  (191 other events, 405.3 us)
Sparse Core Ops, SparseCore 0:
  79.5 52.4 all-gather.6
  134.4 63.6 all-gather.4
  641.2 90.2 reduce-scatter.3
where the time goes:
time: 935 us; the launch traced here: 925 us
  Pallas kernels  583 us (62%)
  local copies, waits for them, and re-layouts  99.5 us (11%)
  matrix products  91.8 us (10%)
  waiting for transfers between devices  89.1 us (10%)
  other arithmetic  39.2 us (4%)
  between operations  18.3 us (2%)
    pallas_call x17, Pallas kernels, call(): pl.pallas_call(kernel, out_shape=shapes, in_specs=[pl.BlockSpec(memory_sp...  561 us
    ppermute x1, waiting for transfers between devices, per_device(): w_second_far = lax.ppermute(w_second, 'phase', both_ways)  76 us
    dot_general x24, matrix products, dot(): return jnp.dot(left, right, preferred_element_type=single)  32.6 us
    unnamed x501, local copies, waits for them, and re-layouts  31 us
    dot_general x16, matrix products, t_dot(): lax.dot_general(left, right, (((0,), (0,)), ((), ())), preferred_element_...  29.3 us
    dot_general x16, matrix products, dot_t(): lax.dot_general(left, right, (((1,), (1,)), ((), ())), preferred_element_...  22.6 us
    pallas_call x2, Pallas kernels, by_sequence(): pl.pallas_call(kernel, grid=(PARTS,), out_shape=shapes + total_shapes, in...  22.1 us
  transfers between devices with their start and end apart: 7, of which 2 were waited for; matrix products, arithmetic and copies ran while one was open for 11% of the time, Pallas kernels for 32%

commit v1 on v0

--- a/solution.py
+++ b/solution.py
@@ -357,22 +357,21 @@
     )
 
 
-def rank_sum_kernel(count, extra, *refs):
-    every = count + extra
-    sources, given = refs[:count], refs[count:every]
-    targets, taken = refs[every : every + count], refs[every + count : 2 * every]
+def rank_sum_kernel(count, modes, *refs):
+    every = count + len(modes)
+    sources, team_sources = refs[:count], refs[count:every]
+    targets, team_targets = refs[every : every + count], refs[every + count : 2 * every]
     refs = refs[2 * every :]
     from_core, totals, arrivals = (refs[k * count : (k + 1) * count] for k in range(3))
-    send_sem, recv_sem, give_sem, take_sem = refs[3 * count :]
+    send_sem, recv_sem, *team_sems = refs[3 * count :]
     yh, x, core = lax.axis_index("yh"), lax.axis_index("x"), lax.axis_index("core")
     right, left, far = lax.rem(x + 1, 4), lax.rem(x + 3, 4), lax.rem(x + 2, 4)
     other = 1 - yh
     to_y, to_right, to_left, to_core = {"yh": other}, {"x": right}, {"x": left}, {"core": 1 - core}
     barrier = pltpu.get_barrier_semaphore()
-    to_phase = {"phase": 1 - lax.axis_index("phase")}
-    for device in (to_y, to_right, to_left, to_core, to_phase):
+    for device in (to_y, to_right, to_left, to_core):
         greet(barrier, device)
-    pl.semaphore_wait(barrier, 5)
+    pl.semaphore_wait(barrier, 4 + greet_team(barrier, TEAM))
     items = range(count)
     sent = []
 
@@ -404,9 +403,7 @@
                 to_core,
             )
         )
-    swaps = [
-        send(given[k], taken[k], give_sem.at[k], take_sem.at[k], to_phase) for k in range(extra)
-    ]
+    team = team_copies(TEAM, modes, team_sources, team_targets, *team_sems)
     for item in items:
         landed = from_core[item]
         pltpu.make_async_copy(landed, landed, recv_sem.at[item, 7]).wait()
@@ -443,25 +440,23 @@
         targets[item][...] = (value + arrived(item, 6)).astype(targets[item].dtype)
     for copy in sent:
         copy.wait_send()
-    for copy in swaps:
+    for copy in team:
         copy.wait()
 
 
-def rank_sum(arrays, swapped, number, name):
-    count, extra = len(arrays), len(swapped)
+def rank_sum(arrays, items, number, name):
+    count = len(arrays)
     arrays = [array.reshape((8, 2) + array.shape[1:]) for array in arrays]
     pieces = [array.shape[2:] for array in arrays]
     scratch = [pltpu.VMEM((8,) + piece, brain) for piece in pieces]
     scratch += [pltpu.VMEM((8,) + piece, brain) for piece in pieces]
     scratch += [pltpu.VMEM((7,) + piece, brain) for piece in pieces]
     scratch += [pltpu.SemaphoreType.DMA((count, 8)), pltpu.SemaphoreType.DMA((count, 8))]
-    scratch += [pltpu.SemaphoreType.DMA((extra,)), pltpu.SemaphoreType.DMA((extra,))]
     return call(
-        functools.partial(rank_sum_kernel, count, extra),
-        arrays + swapped,
-        [jax.ShapeDtypeStruct(piece, brain) for piece in pieces]
-        + [jax.ShapeDtypeStruct(array.shape, array.dtype) for array in swapped],
-        scratch,
+        functools.partial(rank_sum_kernel, count, tuple(mode for _, mode in items)),
+        arrays + [array for array, _ in items],
+        [jax.ShapeDtypeStruct(piece, brain) for piece in pieces] + received(TEAM, items),
+        scratch + team_semaphores(TEAM, items),
         number,
         name,
         45,
@@ -784,14 +779,18 @@
     )
     seg_all = seg_got[:, 0, :SEQ]
     sin_got = sin_got[:, :24].reshape(2, 96, 512)
-    w_in, small_all, w_out, sin_all, sout_all, start_all, qkv_got, attn_got = rank_gather(
-        [
-            in_got[:, :12].reshape(96, IN_COLS),
-            small_got.reshape(128, 128),
-            pad_rows(out_proj, 32),
-            sin_got[0],
-            sout_got[0],
-        ],
+
+    def to_other_phase(value):
+        return lax.ppermute(value, "phase", both_ways)
+
+    half = WIDTH // 2
+    w_second_far = to_other_phase(w_second)
+    in_rows, w_second_far = lax.optimization_barrier(
+        (in_got[:, :12].reshape(96, IN_COLS), w_second_far)
+    )
+    w_first_far = [to_other_phase(after(w_first[:half], w_second_far))]
+    w_in, small_all, w_out, start_all, qkv_got, attn_got = rank_gather(
+        [in_rows, small_got.reshape(128, 128), pad_rows(out_proj, 32)],
         [(shuffle(start, mixing), "gather"), (qkv_piece, "swap"), (attn_piece, "zl")],
         1,
         "rank_weights",
@@ -800,8 +799,8 @@
     w_out = w_out[:, :24].reshape(INNER, WIDTH)
     later_wide = jnp.concatenate([qkv_got[:, :12].reshape(96, QKV_COLS), sin_got[1]], axis=1)
     later_tall = jnp.concatenate([attn_got[:, :12].reshape(24, WIDTH), sout_got[1]], axis=0)
-    w_first_far = lax.ppermute(w_first, "phase", both_ways)
-    w_second_far = lax.ppermute(w_second, "phase", both_ways)
+    start_all, first_piece = lax.optimization_barrier((start_all, w_first_far[0]))
+    w_first_far = [first_piece, to_other_phase(after(w_first[half:], first_piece))]
     later_wide = lax.all_gather(later_wide, RANK, axis=0)
     later_tall = lax.all_gather(later_tall, RANK, axis=0)
     w_qkv = later_wide[:, :, :QKV_COLS].reshape(WIDTH, QKV_COLS)
@@ -811,8 +810,6 @@
     def hidden_in(value):
         return value.reshape(16, 4, 24, 512).transpose(1, 0, 2, 3).reshape(WIDTH, 512)
 
-    sin_full = (hidden_in(sin_all), hidden_in(later_wide[:, :, QKV_COLS:]))
-    sout_full = (sout_all.reshape(256, WIDTH), later_tall[:, 24:].reshape(256, WIDTH))
     small_all = small_all.reshape(16, 2, 4, 16, 128)
     router_full = small_all[:, :, :, :12].reshape(16, 2, 4, 24, EXPERTS).transpose(1, 2, 0, 3, 4)
     router_full = router_full.reshape(2, WIDTH, EXPERTS)
@@ -937,8 +934,13 @@
     )
     part = dot(part.reshape(PARTS * SEQ, INNER), w_out)
     part = part.astype(brain).reshape(PARTS, SEQ, WIDTH)
-    part = after(part, (w_first_far, w_second_far))
-    part_got, squares_got = exchange([(part, "swap"), (squares, "swap")], TEAM, 2, "team_mixed_0")
+    part, second_piece = lax.optimization_barrier((part, w_first_far[1]))
+    w_first_far = jnp.concatenate([w_first_far[0], second_piece], axis=0)
+    sin_all, sout_all, part_got, squares_got = rank_gather(
+        [sin_got[0], sout_got[0]], [(part, "swap"), (squares, "swap")], 2, "team_mixed_0"
+    )
+    sin_full = (hidden_in(sin_all), hidden_in(later_wide[:, :, QKV_COLS:]))
+    sout_full = (sout_all.reshape(256, WIDTH), later_tall[:, 24:].reshape(256, WIDTH))
     mean_square = jnp.sum(squares_got[:, 0, :SEQ], axis=0) / DI
     inverse = lax.rsqrt(mean_square + eps)
     mixed0 = jnp.sum(part_got.astype(single), axis=0) * inverse[:, None]
@@ -1030,8 +1032,7 @@
     give_first = t_dot(give_rows, give_both).astype(brain)
     give_second = t_dot(give_hid, give_answer).astype(brain)
     d_rows0, give_first, give_second = lax.optimization_barrier((d_rows0, give_first, give_second))
-    far_first = lax.ppermute(give_first, "phase", both_ways)
-    far_second = lax.ppermute(give_second, "phase", both_ways)
+    far_second = to_other_phase(give_second)
     returned0, d_shared_got0 = expert_exchange(
         [d_rows0], [(d_shared0, "swap")], 14, "collect_back_0"
     )
@@ -1041,9 +1042,14 @@
     d_mixed0 = d_hid0.astype(brain)
     along = jnp.sum(d_mixed0.astype(single) * mixed0, axis=1)
     scalars = jnp.stack([inverse, inverse * inverse * along / DI])
-    d_mixed0, scalars_all = exchange(
-        [(d_mixed0, "gather"), (pad_to(scalars, 8, 128), "gather")], TEAM, 15, "team_dmixed"
-    )
+    d_mixed0, far_second = lax.optimization_barrier((d_mixed0, far_second))
+    sin_part0, sout_part0, d_mixed0, scalars_all = rank_sum(
+        [shared_in_parts(d_sin0), d_sout0.astype(brain).reshape(16, 16, WIDTH)],
+        [(d_mixed0, "gather"), (pad_to(scalars, 8, 128), "gather")],
+        15,
+        "team_dmixed",
+    )
+    far_first = [to_other_phase(after(give_first[:half], d_mixed0))]
     d_mixed0 = d_mixed0.reshape(PARTS * SEQ, WIDTH)
     d_yn = dot_t(d_mixed0, w_out).reshape(PARTS, SEQ, INNER)
     d_zx, yn, core_sums = by_sequence(
@@ -1063,21 +1069,18 @@
     d_skip = jnp.sum(core_sums[5, :INNER].reshape(HEADS_HERE, P_SIZE), axis=1)
     d_step, d_decay = core_sums[7, :HEADS_HERE], core_sums[8, :HEADS_HERE]
     d_w_in = t_dot(n1_all, d_zx)
-    d_n1_part0 = dot_t(d_zx, w_in).astype(brain).reshape(PARTS, SEQ, WIDTH)
-    d_n1_part0, grads_later = lax.optimization_barrier((d_n1_part0, grads_later))
-    (d_n1_got0,) = exchange([(d_n1_part0, "swap")], TEAM, 16, "team_dn1")
-    d_n1_0 = unshuffle(jnp.sum(d_n1_got0.astype(single), axis=0), mixing)
-    d_u0, d_gain00 = jax.vjp(rms_scale, u0, gains[0, 0])[1](d_n1_0)
-    d_u0 = d_u0 + d_hid0
-
-    def keep_and_give(block0, block1):
-        return jnp.where(first_phase, block0, block1), jnp.where(first_phase, block1, block0)
-
-    def by_block(kept, got):
-        return jnp.where(first_phase, jnp.stack([kept, got]), jnp.stack([got, kept]))[None]
-
-    keep_out, give_out = keep_and_give(out0, out1)
-    keep_grad, give_grad = keep_and_give(d_u0, d_u1.astype(single))
+    d_n1_part0 = dot_t(d_zx, w_in).astype(brain)
+    shuffled = start_all.astype(single)
+    shuffled = shuffled * lax.rsqrt(jnp.mean(shuffled * shuffled, axis=-1, keepdims=True) + eps)
+    d_gain00 = jnp.sum(
+        shuffled.reshape(PARTS * SEQ, WIDTH) * d_n1_part0.astype(single), axis=0
+    )
+    d_gain00 = d_gain00.reshape(16, 8, 12).transpose(1, 0, 2).reshape(WIDTH)
+    d_n1_part0 = d_n1_part0.reshape(PARTS, SEQ, WIDTH)
+    d_n1_part0, grads_later, first_piece = lax.optimization_barrier(
+        (d_n1_part0, grads_later, far_first[0])
+    )
+    far_first = [first_piece, to_other_phase(after(give_first[half:], first_piece))]
 
     qkv_part = grads_later[:96, :QKV_COLS].reshape(PARTS, 12, QKV_COLS)
     sin_part1 = grads_later[:96, QKV_COLS:].reshape(4, 24, 512)
@@ -1109,39 +1112,31 @@
     small_grads = jnp.concatenate([d_router, conv_all, gain_all, d_gains, head_all], axis=2)
     small_grads = jnp.pad(small_grads, ((0, 0), (0, 0), (0, 2048 - small_grads.shape[2])))
     small_grads = small_grads.astype(brain).reshape(16, 128, 128)
-    d_outs = jnp.concatenate(
-        [
-            d_w_out.astype(brain).reshape(16, 24, WIDTH),
-            d_sout0.astype(brain).reshape(16, 16, WIDTH),
-            jnp.zeros((16, 8, WIDTH), brain),
-        ],
-        axis=1,
-    )
-    main_part, outs_part, sin_part0, small_part, got_out, got_grad = rank_sum(
+    main_part, out_proj_grad, small_part, d_n1_got0, phase_outputs = rank_sum(
         [
             d_w_in.astype(brain).reshape(16, 96, IN_COLS),
-            d_outs,
-            shared_in_parts(d_sin0),
+            pad_rows(d_w_out.astype(brain).reshape(16, 24, WIDTH), 32),
             small_grads,
         ],
-        [give_out, give_grad],
+        [(d_n1_part0, "swap"), (jnp.stack([out0, out1]), "phase")],
         17,
         "rank_grads",
     )
-    phase_outputs = by_block(keep_out, got_out)
-    input_grads = by_block(keep_grad, got_grad)
     main_part = main_part.reshape(PARTS, 12, IN_COLS)
-    out_proj_grad, sout_part0 = outs_part[:24], outs_part[24:40]
     sin_part0 = sin_part0.reshape(4, 24, 512)
+    d_n1_0 = unshuffle(jnp.sum(d_n1_got0.astype(single), axis=0), mixing)
+    (d_u0,) = jax.vjp(lambda value: rms_scale(value, gains[0, 0]), u0)[1](d_n1_0)
+    d_u0 = d_u0 + d_hid0
 
     rows_kept, d_both_kept, hid_kept, d_answer_kept = (
         jnp.where(first_phase, a, b) for a, b in zip(expert0, expert1)
     )
-    far_first, far_second = after((far_first, far_second), main_part)
+    main_part, second_piece = lax.optimization_barrier((main_part, far_first[1]))
+    far_first = jnp.concatenate([far_first[0], second_piece], axis=0)
     experts_in_grad = t_dot(rows_kept, d_both_kept) + far_first.astype(single)
     experts_out_grad = t_dot(hid_kept, d_answer_kept) + far_second.astype(single)
 
-    main_end, qkv_end, sin_end, sout_end, attn_end, small_end = exchange(
+    main_end, qkv_end, sin_end, sout_end, attn_end, small_end, input_grads = exchange(
         [
             (pad_rows(main_part, 16), "swap"),
             (pad_rows(qkv_part, 16), "swap"),
@@ -1149,6 +1144,7 @@
             (jnp.stack([sout_part0, sout_part1]), "phase"),
             (pad_rows(attn_part, 16), "zl"),
             (small_part.reshape(PARTS, 16, 128), "swap"),
+            (jnp.stack([d_u0, d_u1.astype(single)]), "phase"),
         ],
         TEAM,
         18,
@@ -1190,8 +1186,8 @@
     attn_out_grad = jnp.sum(attn_end[:, :12].astype(single), axis=0)
 
     return (
-        phase_outputs,
-        input_grads,
+        phase_outputs[None],
+        input_grads[None],
         in_proj_grad,
         conv_end[:KW],
         conv_end[KW],
@@ -1199,7 +1195,7 @@
         heads_end[1],
         heads_end[2],
         norm_gain_grad,
-        out_proj_grad.astype(single),
+        out_proj_grad[:24].astype(single),
         query_grad,
         kv_grad,
         attn_out_grad,

time: 935 us -> 894 us (0.956)
  Pallas kernels: 583 us -> 563 us
  waiting for transfers between devices: 89.1 us -> 72.5 us
  other arithmetic: 39.2 us -> 27.2 us
    pallas_call x17 -> x16, Pallas kernels: 561 us -> 540 us  [call(): pl.pallas_call(kernel, out_shape=shapes, in_specs=[pl.BlockSpec(memory_sp...]
    unnamed x4, waiting for transfers between devices: 13 us -> 0.05 us
    ppermute x4 -> x6, waiting for transfers between devices: 76 us -> 72.4 us  [to_other_phase(): return lax.ppermute(value, 'phase', both_ways)]
    unnamed x501 -> x456, local copies, waits for them, and re-layouts: 31 us -> 31.6 us
  transfers between devices with their start and end apart: 7 -> 9, of which waited for: 2 -> 4; matrix products, arithmetic and copies ran while one was open for 11% -> 12% of each run, Pallas kernels for 32% -> 32%
where the time goes in v1:
time: 894 us; the launch traced here: 883 us
  Pallas kernels  563 us (63%)
  matrix products  99.3 us (11%)
  local copies, waits for them, and re-layouts  98.3 us (11%)
  waiting for transfers between devices  72.5 us (8%)
  other arithmetic  27.2 us (3%)
  between operations  17.9 us (2%)
    pallas_call x16, Pallas kernels, call(): pl.pallas_call(kernel, out_shape=shapes, in_specs=[pl.BlockSpec(memory_sp...  540 us
    ppermute x6, waiting for transfers between devices, to_other_phase(): return lax.ppermute(value, 'phase', both_ways)  72.4 us
    dot_general x24, matrix products, dot(): return jnp.dot(left, right, preferred_element_type=single)  33 us
    dot_general x16, matrix products, t_dot(): lax.dot_general(left, right, (((0,), (0,)), ((), ())), preferred_element_...  32.1 us
    unnamed x456, local copies, waits for them, and re-layouts  31.6 us
    dot_general x16, matrix products, dot_t(): lax.dot_general(left, right, (((1,), (1,)), ((), ())), preferred_element_...  26.7 us
    pallas_call x2, Pallas kernels, by_sequence(): pl.pallas_call(kernel, grid=(PARTS,), out_shape=shapes + total_shapes, in...  22.4 us
  transfers between devices with their start and end apart: 9, of which 4 were waited for; matrix products, arithmetic and copies ran while one was open for 12% of the time, Pallas kernels for 32%

profile of v1, /device:TPU:0, one launch (start us, length us, event | category | flops | bytes accessed | tf_op | source)
XLA Modules:
  0.0 883.1 jit_solution(5768214300405199086)
XLA Ops:
  7.3 1.7 collective-permute-start
  13.3 38.9 %team_start.1 = (bf16[8,16,1152]{2,1,0:T(8,128)(2,1)S(1)}, bf16[8,32,512]{2,1,0:T(8,128)(2,1)S(1)}, bf16[2,16,1536]{2,1,0:T(8,128)(2,1)S(1)}, bf16[8,16,128]{2,1,0:T(8,128)(2,1)S(1)}, s32[8,8,128]{2,1,0:T(8,128)S(1)}) custom-call(bf16[8,16,1152]{2,1,0:T(8,128)(2,1)S(1)} %pad.117.refs_0_, bf16[8,32,512]{2,1,0:T(8,128)(2,1)S(1)} %fusion.152.refs_1_, ...), custom_call_target="tpu_custom_call" | custom-call | flops 20000000000 | bytes 1441792 | tf_op jit(solution)/shard_map/team_start/pallas_call | solution.py:151
  54.0 1.9 fusion.45.refs_3_
  56.0 35.4 %rank_weights.1 = (bf16[16,96,1152]{2,1,0:T(8,128)(2,1)}, bf16[16,128,128]{2,1,0:T(8,128)(2,1)S(1)}, bf16[16,32,1536]{2,1,0:T(8,128)(2,1)S(1)}, bf16[8,64,1536]{...) custom-call(bf16[96,1152]{1,0:T(8,128)(2,1)S(1)} %reshape.770.refs_0_, ...), custom_call_target="tpu_custom_call" | custom-call | flops 40000000000 | bytes 14942208 | tf_op jit(solution)/shard_map/rank_weights/pallas_call | solution.py:151
  97.4 3.9 slice_bitcast_fusion
  103.3 1.8 copy.367
  109.2 2.4 slice.335
  116.6 28.4 %collective-permute-done.1 = bf16[768,1024]{1,0:T(8,128)(2,1)} collective-permute-done((bf16[768,1024]{1,0:T(8,128)(2,1)}, bf16[768,1024]{1,0:T(8,128)(2,1)}, u32[]{:S(2)}, u32[]{:S(2)}) %collective-permute-start.1) | collective-permute-done | bytes 1572896 | tf_op jit(solution)/shard_map/ppermute | solution.py:784
  146.1 4.3 fusion.98.zx_ref
  150.5 8.6 mamba_forward.1
  159.0 2.8 constant_dynamic-update-slice_fusion.1
  162.8 1.9 convert_multiply_fusion
  164.7 19.0 %collective-permute-done.2 = bf16[768,1024]{1,0:T(8,128)(2,1)S(1)} collective-permute-done((bf16[768,1024]{1,0:T(8,128)(2,1)S(1)}, bf16[768,1024]{1,0:T(8,128)(2,1)S(1)}, u32[]{:S(2)}, u32[]{:S(2)}) %collective-permute-start.2) | collective-permute-done | bytes 1572896 | tf_op jit(solution)/shard_map/ppermute | solution.py:784
  183.8 34.1 %team_mixed_0.1 = (bf16[16,96,512]{2,1,0:T(8,128)(2,1)S(1)}, bf16[16,16,1536]{2,1,0:T(8,128)(2,1)S(1)}, bf16[8,64,1536]{2,1,0:T(8,128)(2,1)S(1)}, f32[8,8,128]{2,1,0:T(8,128)S(1)}) custom-call(bf16[96,512]{1,0:T(8,128)(2,1)S(1)} %bitcast.564, bf16[16,1536]{1,0:T(8,128)(2,1)S(1)} %get-tuple-element.216.refs_1_, bf16[8,64,1536]{2,1,0:T(8,128)(2,1)S(1)} %bitcast.543, ...), custom_call_target="tpu_custom_call" | custom-call | flops 40000000000 | bytes 7929856 | tf_op jit(solution)/shard_map/team_mixed_0/pallas_call | solution.py:151
  220.2 36.1 %spread_0.1 = (bf16[64,8,1536]{2,1,0:T(8,128)(2,1)S(1)}, bf16[4,64,1536]{2,1,0:T(8,128)(2,1)S(1)}) custom-call(bf16[64,8,1536]{2,1,0:T(8,128)(2,1)S(1)} %fusion.31.refs_0_, bf16[64,1536]{1,0:T(8,128)(2,1)S(1)} %multiply_convert_fusion.6.refs_1_), custom_call_target="tpu_custom_call" | custom-call | flops 40000000000 | bytes 4718592 | tf_op jit(solution)/shard_map/spread_0/pallas_call | solution.py:151
  259.9 3.4 fusion.17
  263.6 1.8 copy-done.205
  267.4 32.0 %collect_0.1 = (bf16[64,8,1536]{2,1,0:T(8,128)(2,1)S(1)}, bf16[4,64,1536]{2,1,0:T(8,128)(2,1)S(1)}) custom-call(bf16[64,8,1536]{2,1,0:T(8,128)(2,1)S(1)} %fusion.33.refs_0_, bf16[4,64,1536]{2,1,0:T(8,128)(2,1)S(1)} %bitcast.558), custom_call_target="tpu_custom_call" | custom-call | flops 40000000000 | bytes 4718592 | tf_op jit(solution)/shard_map/collect_0/pallas_call | solution.py:151
  302.4 1.9 fusion.46.refs_0_
  304.4 16.6 %half_n1.1 = bf16[4,64,1536]{2,1,0:T(8,128)(2,1)S(1)} custom-call(bf16[64,1536]{1,0:T(8,128)(2,1)S(1)} %fusion.46.refs_0_), custom_call_target="tpu_custom_call" | custom-call | flops 20000000000 | bytes 1572864 | tf_op jit(solution)/shard_map/half_n1/pallas_call | solution.py:151
  322.6 2.1 slice.427
  328.1 1.7 slice.415
  329.8 2.3 slice.424
  335.3 12.7 %half_mixed.1 = bf16[4,64,1536]{2,1,0:T(8,128)(2,1)S(1)} custom-call(bf16[4,64,1536]{2,1,0:T(8,128)(2,1)S(1)} %bitcast.547), custom_call_target="tpu_custom_call" | custom-call | flops 20000000000 | bytes 1572864 | tf_op jit(solution)/shard_map/half_mixed/pallas_call | solution.py:151
  349.2 1.8 fusion.32.refs_0_
  353.2 1.8 fusion.36.refs_1_
  355.0 59.3 %spread_1.1 = (bf16[64,8,1536]{2,1,0:T(8,128)(2,1)S(1)}, bf16[64,8,1536]{2,1,0:T(8,128)(2,1)S(1)}, bf16[4,64,1536]{2,1,0:T(8,128)(2,1)S(1)}, bf16[4,64,1536]{2,1,0:T(8,128)(2,1)S(1)}) custom-call(bf16[64,8,1536]{2,1,0:T(8,128)(2,1)} %fusion.32.refs_0_, bf16[64,8,1536]{2,1,0:T(8,128)(2,1)} %fusion.36.refs_1_, ...), custom_call_target="tpu_custom_call" | custom-call | flops 80000000000 | bytes 9437184 | tf_op jit(solution)/shard_map/spread_1/pallas_call | solution.py:151
  418.5 3.5 fusion.15
  422.0 2.8 fusion.179
  424.9 4.5 fusion.34.refs_0_
  430.1 3.1 fusion.30.refs_1_
  433.2 60.4 %collect_1.1 = (bf16[64,8,1536]{2,1,0:T(8,128)(2,1)S(1)}, bf16[64,8,1536]{2,1,0:T(8,128)(2,1)}, bf16[4,64,1536]{2,1,0:T(8,128)(2,1)S(1)}, bf16[4,64,1536]{2,1,0:T(8,128)(2,1)S(1)}) custom-call(bf16[64,8,1536]{2,1,0:T(8,128)(2,1)} %fusion.34.refs_0_, bf16[64,8,1536]{2,1,0:T(8,128)(2,1)} %fusion.30.refs_1_, bf16[4,64,1536]{2,1,0:T(8,128)(2,1)S(1)} %bitcast.554, ...), custom_call_target="tpu_custom_call" | custom-call | flops 80000000000 | bytes 9437184 | tf_op jit(solution)/shard_map/collect_1/pallas_call | solution.py:151
  498.1 13.0 %half_dmixed.1 = bf16[4,64,1536]{2,1,0:T(8,128)(2,1)S(1)} custom-call(bf16[64,1536]{1,0:T(8,128)(2,1)S(1)} %fusion.261.refs_0_), custom_call_target="tpu_custom_call" | custom-call | flops 20000000000 | bytes 1572864 | tf_op jit(solution)/shard_map/half_dmixed/pallas_call | solution.py:151
  519.9 2.1 reshape.825
  525.4 3.4 reshape.829
  530.8 3.6 pad_maximum_fusion
  534.4 2.4 convolution_convert_fusion.13
  536.8 13.7 %half_dn1.1 = bf16[4,64,1536]{2,1,0:T(8,128)(2,1)S(1)} custom-call(bf16[4,64,1536]{2,1,0:T(8,128)(2,1)S(1)} %bitcast.570), custom_call_target="tpu_custom_call" | custom-call | flops 20000000000 | bytes 1572864 | tf_op jit(solution)/shard_map/half_dn1/pallas_call | solution.py:151
  551.2 2.0 fusion.1
  555.8 32.9 %spread_back_0.1 = (bf16[64,8,1536]{2,1,0:T(8,128)(2,1)S(1)}, bf16[4,64,1536]{2,1,0:T(8,128)(2,1)S(1)}) custom-call(bf16[64,8,1536]{2,1,0:T(8,128)(2,1)S(1)} %fusion.35.refs_0_, bf16[64,1536]{1,0:T(8,128)(2,1)S(1)} %get-tuple-element.184.refs_1_), custom_call_target="tpu_custom_call" | custom-call | flops 40000000000 | bytes 4718592 | tf_op jit(solution)/shard_map/spread_back_0/pallas_call | solution.py:151
  588.8 2.1 convolution_convert_fusion.2
  595.3 3.5 convolution_convert_fusion
  598.9 1.9 fusion.27
  605.2 32.5 %collect_back_0.1 = (bf16[64,8,1536]{2,1,0:T(8,128)(2,1)S(1)}, bf16[4,64,1536]{2,1,0:T(8,128)(2,1)S(1)}) custom-call(bf16[64,8,1536]{2,1,0:T(8,128)(2,1)S(1)} %bitcast.568, bf16[4,64,1536]{2,1,0:T(8,128)(2,1)S(1)} %bitcast.557), custom_call_target="tpu_custom_call" | custom-call | flops 40000000000 | bytes 4718592 | tf_op jit(solution)/shard_map/collect_back_0/pallas_call | solution.py:151
  639.7 1.7 collective-permute-start.3
  641.5 2.1 fusion.54
  645.3 2.0 stack.115
  647.3 1.9 copy.395
  649.2 2.0 stack.116
  656.1 2.0 fusion.267
  659.7 2.7 fusion.51
  663.2 2.0 copy.400
  666.4 11.6 %collective-permute-done.3 = bf16[512,1536]{1,0:T(8,128)(2,1)} collective-permute-done((bf16[512,1536]{1,0:T(8,128)(2,1)}, bf16[512,1536]{1,0:T(8,128)(2,1)}, u32[]{:S(2)}, u32[]{:S(2)}) %collective-permute-start.3) | collective-permute-done | bytes 1572896 | tf_op jit(solution)/shard_map/ppermute | solution.py:784
  678.0 38.3 %team_dmixed.1 = (bf16[96,512]{1,0:T(8,128)(2,1)S(1)}, bf16[16,1536]{1,0:T(8,128)(2,1)S(1)}, bf16[8,64,1536]{2,1,0:T(8,128)(2,1)S(1)}, f32[8,8,128]{2,1,0:T(8,128)S(1)}) custom-call(bf16[8,2,96,512]{3,2,1,0:T(8,128)(2,1)S(1)} %bitcast.541, bf16[8,2,16,1536]{3,2,1,0:T(8,128)(2,1)S(1)} %bitcast.555, bf16[64,1536]{1,0:T(8,128)(2,1)S(1)} %get-tuple-element.136.refs_2_, ...), custom_call_target="tpu_custom_call" | custom-call | flops 44999999488 | bytes 3506176 | tf_op jit(solution)/shard_map/team_dmixed/pallas_call | solution.py:151
  718.6 13.9 %mamba_backward.1 = (bf16[8,64,1152]{2,1,0:T(8,128)(2,1)S(1)}, bf16[8,64,384]{2,1,0:T(8,128)(2,1)S(1)}, f32[16,640]{1,0:T(8,128)S(1)}) custom-call(f32[8,64,1152]{2,1,0:T(8,128)S(1)} %copy-done.7, f32[8,64,64]{2,1,0:T(8,128)S(1)} %and_convert_fusion.masks_ref, f32[8,64,128]{2,1,0:T(8,128)S(1)} %copy-done.15, f32[8,640]{1,0:T(8,128)S(1)} %copy-done.30, ...), custom_call_target="tpu_custom_call" | custom-call | tf_op jit(solution)/shard_map/mamba_backward/pallas_call | solution.py:684
  733.1 6.5 fusion.12
  739.9 3.2 fusion.29
  746.5 4.6 add_bitcast_fusion.1
  751.1 4.2 fusion.5
  755.3 13.4 %collective-permute-done.4 = bf16[768,1024]{1,0:T(8,128)(2,1)} collective-permute-done((bf16[768,1024]{1,0:T(8,128)(2,1)}, bf16[768,1024]{1,0:T(8,128)(2,1)}, u32[]{:S(2)}, u32[]{:S(2)}) %collective-permute-start.4) | collective-permute-done | bytes 1572896 | tf_op jit(solution)/shard_map/ppermute | solution.py:784
  769.0 65.2 %rank_grads.1 = (bf16[96,1152]{1,0:T(8,128)(2,1)S(1)}, bf16[32,1536]{1,0:T(8,128)(2,1)S(1)}, bf16[128,128]{1,0:T(8,128)(2,1)S(1)}, bf16[8,64,1536]{2,1,0:T(8,128)(2,1)S(1)}, bf16[2,64,1536]{2,1,0:T(8,128)(2,1)S(1)}) custom-call(bf16[8,2,96,1152]{3,2,1,0:T(8,128)(2,1)} %bitcast.667, bf16[8,2,32,1536]{3,2,1,0:T(8,128)(2,1)S(1)} %bitcast.540, ...), custom_call_target="tpu_custom_call" | custom-call | flops 44999999488 | bytes 4636672 | tf_op jit(solution)/shard_map/rank_grads/pallas_call | solution.py:151
  835.0 2.0 fusion
  840.7 19.2 %team_end.1 = (bf16[8,16,1152]{2,1,0:T(8,128)(2,1)S(1)}, bf16[8,16,640]{2,1,0:T(8,128)(2,1)S(1)}, bf16[8,32,512]{2,1,0:T(8,128)(2,1)S(1)}, bf16[2,16,1536]{2,1,0...) custom-call(bf16[8,16,1152]{2,1,0:T(8,128)(2,1)S(1)} %pad.144.refs_0, ...), custom_call_target="tpu_custom_call" | custom-call | flops 20000000000 | bytes 3473408 | tf_op jit(solution)/shard_map/team_end/pallas_call | solution.py:151
  861.9 5.4 add_bitcast_fusion
  (759 shorter events, 115.4 us)
Async XLA Ops:
  7.2 46.7 %copy-start = (s32[2,64,6]{1,0,2:T(2,128)S(1)}, s32[2,64,6]{1,0,2:T(2,128)}, u32[]{:S(2)}) copy-start(s32[2,64,6]{1,0,2:T(2,128)} %param.24) | copy-start | bytes 9220
  7.3 313.7 %all-gather.7.cloned.1.call-start = ((), (), s32[]{:S(2)}) async-start(), calls=%async_computation.2 | async-start | bytes 2088960 | tf_op jit(solution)/shard_map/all_gather | solution.py:805
  7.3 48.6 %collective-permute-start = (bf16[512,1536]{1,0:T(8,128)(2,1)}, bf16[512,1536]{1,0:T(8,128)(2,1)}, u32[]{:S(2)}, u32[]{:S(2)}) collective-permute-start(bf16[512,1536]{1,0:T(8,128)(2,1)} %bitcast.664), channel_id=1, source_target_pairs={{0,64},{64,0},{1,65},{65,1},{2,66},{66,2},{3,67},{67,3},{4,68},{68... | collective-permute-start | bytes 4718600 | tf_op jit(solution)/shard_map/ppermute | solution.py:784
  13.2 39.2 %copy-start.148 = (bf16[12,1536]{1,0:T(8,128)(2,1)S(1)}, bf16[12,1536]{1,0:T(8,128)(2,1)}, u32[]{:S(2)}) copy-start(bf16[12,1536]{1,0:T(8,128)(2,1)} %param.33) | copy-start | bytes 110596
  13.3 39.2 %copy-start.154 = (bf16[12,1024]{1,0:T(8,128)(2,1)S(1)}, bf16[12,1024]{1,0:T(8,128)(2,1)}, u32[]{:S(2)}) copy-start(bf16[12,1024]{1,0:T(8,128)(2,1)} %param.34) | copy-start | bytes 73732
  54.0 248.4 %copy-start.168 = (s32[1536]{0:T(1024)}, s32[1536]{0:T(1024)S(1)}, u32[]{:S(2)}) copy-start(s32[1536]{0:T(1024)S(1)} %fusion.209) | copy-start | bytes 18436
  55.9 39.2 %copy-start.198 = (f32[48]{0:T(128)S(1)}, f32[48]{0:T(128)}, u32[]{:S(2)}) copy-start(f32[48]{0:T(128)} %param.29) | copy-start | bytes 580
  56.0 39.2 %copy-start.199 = (f32[48]{0:T(128)S(1)}, f32[48]{0:T(128)}, u32[]{:S(2)}) copy-start(f32[48]{0:T(128)} %param.28) | copy-start | bytes 580
  92.5 70.3 %copy-start.8 = (bf16[8,64,1536]{2,1,0:T(8,128)(2,1)}, bf16[8,64,1536]{2,1,0:T(8,128)(2,1)S(1)}, u32[]{:S(2)}) copy-start(bf16[8,64,1536]{2,1,0:T(8,128)(2,1)S(1)} %get-tuple-element.99) | copy-start | bytes 4718596
  93.3 234.8 %all-gather.5.cloned.1.call-start = ((), (), s32[]{:S(2)}) async-start(), calls=%async_computation.1 | async-start | bytes 3760128 | tf_op jit(solution)/shard_map/all_gather | solution.py:804
  93.5 257.8 %copy-start.119 = (pred[64,64]{0,1:T(32,128)(4,1)}, pred[64,64]{0,1:T(32,128)(4,1)S(1)}, u32[]{:S(2)}) copy-start(pred[64,64]{0,1:T(32,128)(4,1)S(1)} %copy.382) | copy-start | bytes 12292
  95.2 55.2 %copy-start.35 = (f32[8,128]{1,0:T(8,128)}, f32[8,128]{1,0:T(8,128)S(1)}, u32[]{:S(2)}) copy-start(f32[8,128]{1,0:T(8,128)S(1)} %select_maximum_fusion.1.heads_ref) | copy-start | bytes 12292
  95.3 55.2 %copy-start.14 = (f32[8,64,128]{2,1,0:T(8,128)}, f32[8,64,128]{2,1,0:T(8,128)S(1)}, u32[]{:S(2)}) copy-start(f32[8,64,128]{2,1,0:T(8,128)S(1)} %pad_convert_fusion.same_ref) | copy-start | bytes 786436
  95.6 256.9 %copy-start.80 = (pred[64,512]{1,0:T(32,128)(4,1)}, pred[64,512]{1,0:T(32,128)(4,1)S(1)}, u32[]{:S(2)}) copy-start(pred[64,512]{1,0:T(32,128)(4,1)S(1)} %convolution_compare_fusion) | copy-start | bytes 98308
  101.3 43.6 %collective-permute-start.1 = (bf16[768,1024]{1,0:T(8,128)(2,1)}, bf16[768,1024]{1,0:T(8,128)(2,1)}, u32[]{:S(2)}, u32[]{:S(2)}) collective-permute-start(bf16[768,1024]{1,0:T(8,128)(2,1)} %get-tuple-element.98), channel_id=1, source_target_pairs={{0,64},{64,0},{1,65},{65,1},{2,66},{66,2},{3,67},{67,3},{4,68},{68... | collective-permute-start | bytes 4718600 | tf_op jit(solution)/shard_map/ppermute | solution.py:784
  107.3 159.2 %copy-start.132 = (f32[1536]{0:T(1024)}, f32[1536]{0:T(1024)S(1)}, u32[]{:S(2)}) copy-start(f32[1536]{0:T(1024)S(1)} %get-tuple-element.179) | copy-start | bytes 18436
  107.3 195.1 %copy-start.143 = (f32[1536]{0:T(1024)}, f32[1536]{0:T(1024)S(1)}, u32[]{:S(2)}) copy-start(f32[1536]{0:T(1024)S(1)} %get-tuple-element.178) | copy-start | bytes 18436
  109.0 37.1 %copy-start.166 = (f32[1536]{0:T(1024)}, f32[1536]{0:T(1024)S(1)}, u32[]{:S(2)}) copy-start(f32[1536]{0:T(1024)S(1)} %convert_element_type.678) | copy-start | bytes 18436
  116.4 652.3 %reduce-scatter.4.cloned.1.call-start = ((), (), s32[]{:S(2)}) async-start(), calls=%async_computation.3 | async-start | bytes 5953536
  116.5 28.9 %copy-start.101 = (bf16[768,1024]{1,0:T(8,128)(2,1)S(1)}, bf16[768,1024]{1,0:T(8,128)(2,1)}, u32[]{:S(2)}) copy-start(bf16[768,1024]{1,0:T(8,128)(2,1)} %get-tuple-element.108) | copy-start | bytes 4718596
  116.6 33.9 %copy-start.29 = (f32[8,640]{1,0:T(8,128)}, f32[8,640]{1,0:T(8,128)S(1)}, u32[]{:S(2)}) copy-start(f32[8,640]{1,0:T(8,128)S(1)} %maximum_maximum_fusion.taps_ref) | copy-start | bytes 61444
  145.3 17.4 %copy-start.157 = (f32[8,64]{1,0:T(8,128)}, f32[8,64]{1,0:T(8,128)S(1)}, u32[]{:S(2)}) copy-start(f32[8,64]{1,0:T(8,128)S(1)} %add_rsqrt_fusion) | copy-start | bytes 6148
  145.4 38.4 %collective-permute-start.2 = (bf16[768,1024]{1,0:T(8,128)(2,1)S(1)}, bf16[768,1024]{1,0:T(8,128)(2,1)S(1)}, u32[]{:S(2)}, u32[]{:S(2)}) collective-permute-start(bf16[768,1024]{1,0:T(8,128)(2,1)S(1)} %copy-done.101), channel_id=1, source_target_pairs={{0,64},{64,0},{1,65},{65,1},{2,66},{66,2},{3,67},{67,3},{4,68},{68... | collective-permute-start | bytes 4718600 | tf_op jit(solution)/shard_map/ppermute | solution.py:784
  150.5 11.3 %copy-start.6 = (f32[8,64,1152]{2,1,0:T(8,128)}, f32[8,64,1152]{2,1,0:T(8,128)S(1)}, u32[]{:S(2)}) copy-start(f32[8,64,1152]{2,1,0:T(8,128)S(1)} %fusion.98.zx_ref) | copy-start | bytes 7077892
  183.8 115.8 %copy-start.93 = (bf16[768,1024]{1,0:T(8,128)(2,1)}, bf16[768,1024]{1,0:T(8,128)(2,1)S(1)}, u32[]{:S(2)}) copy-start(bf16[768,1024]{1,0:T(8,128)(2,1)S(1)} %collective-permute-done.2) | copy-start | bytes 4718596
  217.9 49.1 %copy-start.25 = (bf16[16,16,1536]{2,1,0:T(8,128)(2,1)}, bf16[16,16,1536]{2,1,0:T(8,128)(2,1)S(1)}, u32[]{:S(2)}) copy-start(bf16[16,16,1536]{2,1,0:T(8,128)(2,1)S(1)} %get-tuple-element.117) | copy-start | bytes 2359300
  218.2 48.3 %copy-start.57 = (f32[64,1536]{1,0:T(8,128)}, f32[64,1536]{1,0:T(8,128)S(1)}, u32[]{:S(2)}) copy-start(f32[64,1536]{1,0:T(8,128)S(1)} %convert_reduce_fusion.1) | copy-start | bytes 1179652
  218.7 47.8 %copy-start.176 = (f32[64]{0:T(128)}, f32[64]{0:T(128)S(1)}, u32[]{:S(2)}) copy-start(f32[64]{0:T(128)S(1)} %get-tuple-element.226) | copy-start | bytes 772
  219.4 37.0 %copy-start.194 = (f32[64]{0:T(128)}, f32[64]{0:T(128)S(1)}, u32[]{:S(2)}) copy-start(f32[64]{0:T(128)S(1)} %get-tuple-element.191) | copy-start | bytes 772
  219.5 82.3 %copy-start.52 = (f32[64,1536]{1,0:T(8,128)}, f32[64,1536]{1,0:T(8,128)S(1)}, u32[]{:S(2)}) copy-start(f32[64,1536]{1,0:T(8,128)S(1)} %get-tuple-element.192) | copy-start | bytes 1179652
  219.5 47.0 %copy-start.161 = (f32[64]{0:T(128)}, f32[64]{0:T(128)S(1)}, u32[]{:S(2)}) copy-start(f32[64]{0:T(128)S(1)} %fusion.235) | copy-start | bytes 772
  219.6 36.8 %copy-start.16 = (bf16[64,1536]{1,0:T(8,128)(2,1)}, bf16[64,1536]{1,0:T(8,128)(2,1)S(1)}, u32[]{:S(2)}) copy-start(bf16[64,1536]{1,0:T(8,128)(2,1)S(1)} %multiply_convert_fusion.6.refs_1_) | copy-start | bytes 589828
  258.4 8.6 copy-start.106
  267.0 32.7 %copy-start.123 = (f32[64,64]{0,1:T(8,128)}, f32[64,64]{0,1:T(8,128)S(1)}, u32[]{:S(2)}) copy-start(f32[64,64]{0,1:T(8,128)S(1)} %get-tuple-element.228) | copy-start | bytes 49156
  267.0 32.7 %copy-start.171 = (f32[64]{0:T(128)}, f32[64]{0:T(128)S(1)}, u32[]{:S(2)}) copy-start(f32[64]{0:T(128)S(1)} %get-tuple-element.227) | copy-start | bytes 772
  267.0 32.7 %copy-start.177 = (f32[64]{0:T(128)}, f32[64]{0:T(128)S(1)}, u32[]{:S(2)}) copy-start(f32[64]{0:T(128)S(1)} %fusion.195) | copy-start | bytes 772
  267.4 32.1 %copy-start.113 = (bf16[1536,1024]{1,0:T(8,128)(2,1)S(1)}, bf16[1536,1024]{1,0:T(8,128)(2,1)}, u32[]{:S(2)}) copy-start(bf16[1536,1024]{1,0:T(8,128)(2,1)} %constant_dynamic-update-slice_fusion.1) | copy-start | bytes 9437188
  302.3 45.8 %copy-start.60 = (bf16[64,1536]{1,0:T(8,128)(2,1)}, bf16[64,1536]{1,0:T(8,128)(2,1)S(1)}, u32[]{:S(2)}) copy-start(bf16[64,1536]{1,0:T(8,128)(2,1)S(1)} %get-tuple-element.230) | copy-start | bytes 589828
  320.9 11.1 %copy-start.39 = (bf16[4,64,1536]{2,1,0:T(8,128)(2,1)}, bf16[4,64,1536]{2,1,0:T(8,128)(2,1)S(1)}, u32[]{:S(2)}) copy-start(bf16[4,64,1536]{2,1,0:T(8,128)(2,1)S(1)} %half_n1.1) | copy-start | bytes 2359300
  334.4 13.6 %copy-start.90 = (bf16[4,64,3,128]{3,2,1,0:T(4,128)(2,1)}, bf16[4,64,3,128]{3,2,1,0:T(4,128)(2,1)S(1)}, u32[]{:S(2)}) copy-start(bf16[4,64,3,128]{3,2,1,0:T(4,128)(2,1)S(1)} %copy.377) | copy-start | bytes 589828
  414.3 7.7 copy-start.19
  433.1 60.5 %copy-start.81 = (pred[64,512]{1,0:T(32,128)(4,1)S(1)}, pred[64,512]{1,0:T(32,128)(4,1)}, u32[]{:S(2)}) copy-start(pred[64,512]{1,0:T(32,128)(4,1)} %copy-done.80) | copy-start | bytes 98308
  498.1 13.0 %copy-start.65 = (bf16[3,128,1536,1]{2,1,0,3:T(8,128)(2,1)S(1)}, bf16[3,128,1536,1]{2,1,0,3:T(8,128)(2,1)}, u32[]{:S(2)}) copy-start(bf16[3,128,1536,1]{2,1,0,3:T(8,128)(2,1)} %reshape.886) | copy-start | bytes 3538948
  555.8 32.9 %copy-start.20 = (bf16[64,8,1536]{2,1,0:T(8,128)(2,1)S(1)}, bf16[64,8,1536]{2,1,0:T(8,128)(2,1)}, u32[]{:S(2)}) copy-start(bf16[64,8,1536]{2,1,0:T(8,128)(2,1)} %copy-done.19) | copy-start | bytes 4718596
  555.8 32.9 %copy-start.87 = (bf16[512,512]{1,0:T(8,128)(2,1)S(1)}, bf16[512,512]{1,0:T(8,128)(2,1)}, u32[]{:S(2)}) copy-start(bf16[512,512]{1,0:T(8,128)(2,1)} %copy-done.86) | copy-start | bytes 1572868
  555.8 32.9 %copy-start.128 = (bf16[512,512]{1,0:T(8,128)(2,1)S(1)}, bf16[512,512]{1,0:T(8,128)(2,1)}, u32[]{:S(2)}) copy-start(bf16[512,512]{1,0:T(8,128)(2,1)} %copy-done.127) | copy-start | bytes 1572868
  588.7 14.3 %copy-start.27 = (bf16[4,64,1536]{2,1,0:T(8,128)(2,1)}, bf16[4,64,1536]{2,1,0:T(8,128)(2,1)S(1)}, u32[]{:S(2)}) copy-start(bf16[4,64,1536]{2,1,0:T(8,128)(2,1)S(1)} %get-tuple-element.130) | copy-start | bytes 2359300
  603.5 34.2 %copy-start.107 = (f32[256,256]{1,0:T(8,128)}, f32[256,256]{1,0:T(8,128)S(1)}, u32[]{:S(2)}) copy-start(f32[256,256]{1,0:T(8,128)S(1)} %get-tuple-element.202) | copy-start | bytes 786436
  603.5 34.2 %copy-start.109 = (f32[256,256]{1,0:T(8,128)}, f32[256,256]{1,0:T(8,128)S(1)}, u32[]{:S(2)}) copy-start(f32[256,256]{1,0:T(8,128)S(1)} %get-tuple-element.203) | copy-start | bytes 786436
  605.2 32.7 %copy-start.53 = (f32[64,1536]{1,0:T(8,128)S(1)}, f32[64,1536]{1,0:T(8,128)}, u32[]{:S(2)}) copy-start(f32[64,1536]{1,0:T(8,128)} %copy-done.52) | copy-start | bytes 1179652
  605.2 32.7 %copy-start.133 = (f32[1536]{0:T(1024)S(1)}, f32[1536]{0:T(1024)}, u32[]{:S(2)}) copy-start(f32[1536]{0:T(1024)} %copy-done.132) | copy-start | bytes 18436
  605.2 32.7 %copy-start.162 = (f32[64]{0:T(128)S(1)}, f32[64]{0:T(128)}, u32[]{:S(2)}) copy-start(f32[64]{0:T(128)} %copy-done.161) | copy-start | bytes 772
  639.7 38.3 %collective-permute-start.3 = (bf16[512,1536]{1,0:T(8,128)(2,1)}, bf16[512,1536]{1,0:T(8,128)(2,1)}, u32[]{:S(2)}, u32[]{:S(2)}) collective-permute-start(bf16[512,1536]{1,0:T(8,128)(2,1)} %convolution_convert_fusion.2), channel_id=1, source_target_pairs={{0,64},{64,0},{1,65},{65,1},{2,66},{66,2},{3,67},{67,3},{4,68},{68... | collective-permute-start | bytes 4718600 | tf_op jit(solution)/shard_map/ppermute | solution.py:784
  645.3 7.3 copy-start.122
  678.0 38.3 %copy-start.64 = (bf16[16,24,1536]{2,1,0:T(8,128)(2,1)S(1)}, bf16[16,24,1536]{2,1,0:T(8,128)(2,1)}, u32[]{:S(2)}) copy-start(bf16[16,24,1536]{2,1,0:T(8,128)(2,1)} %slice.335) | copy-start | bytes 3538948
  716.3 16.2 %copy-start.41 = (bf16[8,64,1536]{2,1,0:T(8,128)(2,1)}, bf16[8,64,1536]{2,1,0:T(8,128)(2,1)S(1)}, u32[]{:S(2)}) copy-start(bf16[8,64,1536]{2,1,0:T(8,128)(2,1)S(1)} %get-tuple-element.137) | copy-start | bytes 4718596
  732.5 7.1 copy-start.37
  732.5 36.2 %collective-permute-start.4 = (bf16[768,1024]{1,0:T(8,128)(2,1)}, bf16[768,1024]{1,0:T(8,128)(2,1)}, u32[]{:S(2)}, u32[]{:S(2)}) collective-permute-start(bf16[768,1024]{1,0:T(8,128)(2,1)} %get-tuple-element.144), channel_id=1, source_target_pairs={{0,64},{64,0},{1,65},{65,1},{2,66},{66,2},{3,67},{67,3},{4,68},{68... | collective-permute-start | bytes 4718600 | tf_op jit(solution)/shard_map/ppermute | solution.py:784
  768.8 71.9 %collective-permute-start.5 = (bf16[768,1024]{1,0:T(8,128)(2,1)}, bf16[768,1024]{1,0:T(8,128)(2,1)}, u32[]{:S(2)}, u32[]{:S(2)}) collective-permute-start(bf16[768,1024]{1,0:T(8,128)(2,1)} %get-tuple-element.150), channel_id=1, source_target_pairs={{0,64},{64,0},{1,65},{65,1},{2,66},{66,2},{3,67},{67,3},{4,68},{68... | collective-permute-start | bytes 4718600 | tf_op jit(solution)/shard_map/ppermute | solution.py:784
  840.7 21.2 %copy-start.47 = (bf16[64,8,1536]{2,1,0:T(8,128)(2,1)S(1)}, bf16[64,8,1536]{2,1,0:T(8,128)(2,1)}, u32[]{:S(2)}) copy-start(bf16[64,8,1536]{2,1,0:T(8,128)(2,1)} %copy-done.45) | copy-start | bytes 4718596
  840.7 21.2 %copy-start.216 = (f32[512,512]{1,0:T(8,128)S(1)}, f32[512,512]{1,0:T(8,128)}, u32[]{:S(2)}) copy-start(f32[512,512]{1,0:T(8,128)} %copy-done.214) | copy-start | bytes 3145732
  840.7 21.2 %copy-start.218 = (f32[512,512]{1,0:T(8,128)S(1)}, f32[512,512]{1,0:T(8,128)}, u32[]{:S(2)}) copy-start(f32[512,512]{1,0:T(8,128)} %copy-done.217) | copy-start | bytes 3145732
  840.7 21.2 %copy-start.220 = (f32[512,512]{1,0:T(8,128)S(1)}, f32[512,512]{1,0:T(8,128)}, u32[]{:S(2)}) copy-start(f32[512,512]{1,0:T(8,128)} %copy-done.219) | copy-start | bytes 3145732
  860.1 7.2 copy-start.121
  (170 other events, 379.0 us)
Sparse Core Ops, SparseCore 0:
  93.4 57.1 all-gather.6
  153.6 63.6 all-gather.4
  641.6 98.0 reduce-scatter.3

commit v2 on v1

--- a/solution.py
+++ b/solution.py
@@ -783,12 +783,18 @@
     def to_other_phase(value):
         return lax.ppermute(value, "phase", both_ways)
 
+    def in_turn(value, count=3):
+        pieces = []
+        for piece in jnp.split(value, count, axis=0):
+            pieces.append(to_other_phase(after(piece, pieces[-1]) if pieces else piece))
+        return pieces
+
     half = WIDTH // 2
     w_second_far = to_other_phase(w_second)
     in_rows, w_second_far = lax.optimization_barrier(
         (in_got[:, :12].reshape(96, IN_COLS), w_second_far)
     )
-    w_first_far = [to_other_phase(after(w_first[:half], w_second_far))]
+    first_pieces = in_turn(after(w_first[:half], w_second_far))
     w_in, small_all, w_out, start_all, qkv_got, attn_got = rank_gather(
         [in_rows, small_got.reshape(128, 128), pad_rows(out_proj, 32)],
         [(shuffle(start, mixing), "gather"), (qkv_piece, "swap"), (attn_piece, "zl")],
@@ -799,8 +805,8 @@
     w_out = w_out[:, :24].reshape(INNER, WIDTH)
     later_wide = jnp.concatenate([qkv_got[:, :12].reshape(96, QKV_COLS), sin_got[1]], axis=1)
     later_tall = jnp.concatenate([attn_got[:, :12].reshape(24, WIDTH), sout_got[1]], axis=0)
-    start_all, first_piece = lax.optimization_barrier((start_all, w_first_far[0]))
-    w_first_far = [first_piece, to_other_phase(after(w_first[half:], first_piece))]
+    start_all, first_pieces = lax.optimization_barrier((start_all, first_pieces))
+    second_pieces = in_turn(after(w_first[half:], first_pieces[-1]))
     later_wide = lax.all_gather(later_wide, RANK, axis=0)
     later_tall = lax.all_gather(later_tall, RANK, axis=0)
     w_qkv = later_wide[:, :, :QKV_COLS].reshape(WIDTH, QKV_COLS)
@@ -934,8 +940,8 @@
     )
     part = dot(part.reshape(PARTS * SEQ, INNER), w_out)
     part = part.astype(brain).reshape(PARTS, SEQ, WIDTH)
-    part, second_piece = lax.optimization_barrier((part, w_first_far[1]))
-    w_first_far = jnp.concatenate([w_first_far[0], second_piece], axis=0)
+    part, second_pieces = lax.optimization_barrier((part, second_pieces))
+    w_first_far = jnp.concatenate(first_pieces + second_pieces, axis=0)
     sin_all, sout_all, part_got, squares_got = rank_gather(
         [sin_got[0], sout_got[0]], [(part, "swap"), (squares, "swap")], 2, "team_mixed_0"
     )
@@ -1049,7 +1055,7 @@
         15,
         "team_dmixed",
     )
-    far_first = [to_other_phase(after(give_first[:half], d_mixed0))]
+    far_first = in_turn(after(give_first[:half], d_mixed0))
     d_mixed0 = d_mixed0.reshape(PARTS * SEQ, WIDTH)
     d_yn = dot_t(d_mixed0, w_out).reshape(PARTS, SEQ, INNER)
     d_zx, yn, core_sums = by_sequence(
@@ -1077,10 +1083,10 @@
     )
     d_gain00 = d_gain00.reshape(16, 8, 12).transpose(1, 0, 2).reshape(WIDTH)
     d_n1_part0 = d_n1_part0.reshape(PARTS, SEQ, WIDTH)
-    d_n1_part0, grads_later, first_piece = lax.optimization_barrier(
-        (d_n1_part0, grads_later, far_first[0])
-    )
-    far_first = [first_piece, to_other_phase(after(give_first[half:], first_piece))]
+    d_n1_part0, grads_later, first_pieces = lax.optimization_barrier(
+        (d_n1_part0, grads_later, far_first)
+    )
+    second_piece = to_other_phase(after(give_first[half:], first_pieces[-1]))
 
     qkv_part = grads_later[:96, :QKV_COLS].reshape(PARTS, 12, QKV_COLS)
     sin_part1 = grads_later[:96, QKV_COLS:].reshape(4, 24, 512)
@@ -1131,8 +1137,8 @@
     rows_kept, d_both_kept, hid_kept, d_answer_kept = (
         jnp.where(first_phase, a, b) for a, b in zip(expert0, expert1)
     )
-    main_part, second_piece = lax.optimization_barrier((main_part, far_first[1]))
-    far_first = jnp.concatenate([far_first[0], second_piece], axis=0)
+    main_part, second_piece = lax.optimization_barrier((main_part, second_piece))
+    far_first = jnp.concatenate(first_pieces + [second_piece], axis=0)
     experts_in_grad = t_dot(rows_kept, d_both_kept) + far_first.astype(single)
     experts_out_grad = t_dot(hid_kept, d_answer_kept) + far_second.astype(single)
 

time: 894 us -> 920 us (1.029)
  local copies, waits for them, and re-layouts: 98.3 us -> 123 us
  starting transfers between devices: 5.35 us -> 25.7 us
  Pallas kernels: 563 us -> 550 us
    ppermute x6 -> x12, starting transfers between devices: 5.24 us -> 25.6 us  [to_other_phase(): return lax.ppermute(value, 'phase', both_ways)]
    unnamed x456 -> x467, local copies, waits for them, and re-layouts: 31.6 us -> 45.3 us
    pallas_call x16, Pallas kernels: 540 us -> 528 us  [call(): pl.pallas_call(kernel, out_shape=shapes, in_specs=[pl.BlockSpec(memory_sp...]
    ppermute x6 -> x12, waiting for transfers between devices: 72.4 us -> 76.8 us  [to_other_phase(): return lax.ppermute(value, 'phase', both_ways)]
  transfers between devices with their start and end apart: 9 -> 15, of which waited for: 4 -> 9; matrix products, arithmetic and copies ran while one was open for 12% -> 13% of each run, Pallas kernels for 32% -> 29%
where the time goes in v2:
time: 920 us; the launch traced here: 917 us
  Pallas kernels  550 us (60%)
  local copies, waits for them, and re-layouts  123 us (13%)
  matrix products  97.9 us (11%)
  waiting for transfers between devices  76.9 us (8%)
  other arithmetic  26.4 us (3%)
  starting transfers between devices  25.7 us (3%)
  between operations  17.6 us (2%)
    pallas_call x16, Pallas kernels, call(): pl.pallas_call(kernel, out_shape=shapes, in_specs=[pl.BlockSpec(memory_sp...  528 us
    ppermute x12, waiting for transfers between devices, to_other_phase(): return lax.ppermute(value, 'phase', both_ways)  76.8 us
    unnamed x467, local copies, waits for them, and re-layouts  45.3 us
    dot_general x16, matrix products, t_dot(): lax.dot_general(left, right, (((0,), (0,)), ((), ())), preferred_element_...  31.5 us
    dot_general x24, matrix products, dot(): return jnp.dot(left, right, preferred_element_type=single)  28.7 us
    dot_general x16, matrix products, dot_t(): lax.dot_general(left, right, (((1,), (1,)), ((), ())), preferred_element_...  28.3 us
    ppermute x12, starting transfers between devices, to_other_phase(): return lax.ppermute(value, 'phase', both_ways)  25.6 us
    pallas_call x2, Pallas kernels, by_sequence(): pl.pallas_call(kernel, grid=(PARTS,), out_shape=shapes + total_shapes, in...  21.9 us
  transfers between devices with their start and end apart: 15, of which 9 were waited for; matrix products, arithmetic and copies ran while one was open for 13% of the time, Pallas kernels for 29%

profile of v2, /device:TPU:0, one launch (start us, length us, event | category | flops | bytes accessed | tf_op | source)
XLA Modules:
  0.0 917.0 jit_solution(13340942302577080606)
XLA Ops:
  13.3 38.9 %team_start.1 = (bf16[8,16,1152]{2,1,0:T(8,128)(2,1)S(1)}, bf16[8,32,512]{2,1,0:T(8,128)(2,1)S(1)}, bf16[2,16,1536]{2,1,0:T(8,128)(2,1)S(1)}, bf16[8,16,128]{2,1,0:T(8,128)(2,1)S(1)}, s32[8,8,128]{2,1,0:T(8,128)S(1)}) custom-call(bf16[8,16,1152]{2,1,0:T(8,128)(2,1)S(1)} %pad.117.refs_0_, bf16[8,32,512]{2,1,0:T(8,128)(2,1)S(1)} %fusion.152.refs_1_, ...), custom_call_target="tpu_custom_call" | custom-call | flops 20000000000 | bytes 1441792 | tf_op jit(solution)/shard_map/team_start/pallas_call | solution.py:151
  53.7 1.9 fusion.45.refs_3_
  55.7 35.4 %rank_weights.1 = (bf16[16,96,1152]{2,1,0:T(8,128)(2,1)}, bf16[16,128,128]{2,1,0:T(8,128)(2,1)S(1)}, bf16[16,32,1536]{2,1,0:T(8,128)(2,1)S(1)}, bf16[8,64,1536]{...) custom-call(bf16[96,1152]{1,0:T(8,128)(2,1)S(1)} %reshape.778.refs_0_, ...), custom_call_target="tpu_custom_call" | custom-call | flops 40000000000 | bytes 14942208 | tf_op jit(solution)/shard_map/rank_weights/pallas_call | solution.py:151
  97.6 3.9 slice_bitcast_fusion
  101.8 2.5 fusion.268
  105.9 14.3 %collective-permute-done.1 = bf16[256,1024]{1,0:T(8,128)(2,1)} collective-permute-done((bf16[256,1024]{1,0:T(8,128)(2,1)}, bf16[256,1024]{1,0:T(8,128)(2,1)}, u32[]{:S(2)}, u32[]{:S(2)}) %collective-permute-start.1) | collective-permute-done | bytes 524320 | tf_op jit(solution)/shard_map/ppermute | solution.py:784
  126.9 2.4 slice.335
  130.5 1.9 fusion.269
  132.6 1.9 copy.380
  134.4 4.9 collective-permute-done.2
  140.9 9.7 %collective-permute-done.3 = bf16[256,1024]{1,0:T(8,128)(2,1)} collective-permute-done((bf16[256,1024]{1,0:T(8,128)(2,1)}, bf16[256,1024]{1,0:T(8,128)(2,1)}, u32[]{:S(2)}, u32[]{:S(2)}) %collective-permute-start.3) | collective-permute-done | bytes 524320 | tf_op jit(solution)/shard_map/ppermute | solution.py:784
  152.0 11.8 %collective-permute-start.4 = (bf16[256,1024]{1,0:T(8,128)(2,1)S(1)}, bf16[256,1024]{1,0:T(8,128)(2,1)S(1)}, u32[]{:S(2)}, u32[]{:S(2)}) collective-permute-start(bf16[256,1024]{1,0:T(8,128)(2,1)S(1)} %get-tuple-element.231), channel_id=1, source_target_pairs={{0,64},{64,0},{1,65},{65,1},{2,66},{66,2},{3,67},{67,3},{4,68},{68... | collective-permute-start | bytes 1572872 | tf_op jit(solution)/shard_map/ppermute | solution.py:784
  164.2 1.9 constant_dynamic-update-slice_fusion.5
  168.0 2.3 fusion.98.zx_ref
  170.3 2.3 constant_dynamic-update-slice_fusion.3
  172.6 8.1 mamba_forward.1
  186.9 18.1 %collective-permute-done.5 = bf16[256,1024]{1,0:T(8,128)(2,1)S(1)} collective-permute-done((bf16[256,1024]{1,0:T(8,128)(2,1)S(1)}, bf16[256,1024]{1,0:T(8,128)(2,1)S(1)}, u32[]{:S(2)}, u32[]{:S(2)}) %collective-permute-start.5) | collective-permute-done | bytes 524320 | tf_op jit(solution)/shard_map/ppermute | solution.py:784
  205.8 1.9 convert_multiply_fusion
  207.7 6.5 collective-permute-done.6
  214.2 23.0 %team_mixed_0.1 = (bf16[16,96,512]{2,1,0:T(8,128)(2,1)S(1)}, bf16[16,16,1536]{2,1,0:T(8,128)(2,1)S(1)}, bf16[8,64,1536]{2,1,0:T(8,128)(2,1)S(1)}, f32[8,8,128]{2,1,0:T(8,128)S(1)}) custom-call(bf16[96,512]{1,0:T(8,128)(2,1)S(1)} %bitcast.574, bf16[16,1536]{1,0:T(8,128)(2,1)S(1)} %get-tuple-element.249.refs_1_, bf16[8,64,1536]{2,1,0:T(8,128)(2,1)S(1)} %bitcast.551, ...), custom_call_target="tpu_custom_call" | custom-call | flops 40000000000 | bytes 7929856 | tf_op jit(solution)/shard_map/team_mixed_0/pallas_call | solution.py:151
  239.5 38.4 %spread_0.1 = (bf16[64,8,1536]{2,1,0:T(8,128)(2,1)S(1)}, bf16[4,64,1536]{2,1,0:T(8,128)(2,1)S(1)}) custom-call(bf16[64,8,1536]{2,1,0:T(8,128)(2,1)S(1)} %fusion.31.refs_0_, bf16[64,1536]{1,0:T(8,128)(2,1)S(1)} %multiply_convert_fusion.6.refs_1_), custom_call_target="tpu_custom_call" | custom-call | flops 40000000000 | bytes 4718592 | tf_op jit(solution)/shard_map/spread_0/pallas_call | solution.py:151
  281.5 2.9 copy-done.73
  292.8 30.9 %collect_0.1 = (bf16[64,8,1536]{2,1,0:T(8,128)(2,1)S(1)}, bf16[4,64,1536]{2,1,0:T(8,128)(2,1)S(1)}) custom-call(bf16[64,8,1536]{2,1,0:T(8,128)(2,1)S(1)} %fusion.33.refs_0_, bf16[4,64,1536]{2,1,0:T(8,128)(2,1)S(1)} %bitcast.568), custom_call_target="tpu_custom_call" | custom-call | flops 40000000000 | bytes 4718592 | tf_op jit(solution)/shard_map/collect_0/pallas_call | solution.py:151
  326.1 1.9 fusion.46.refs_0_
  328.0 14.1 %half_n1.1 = bf16[4,64,1536]{2,1,0:T(8,128)(2,1)S(1)} custom-call(bf16[64,1536]{1,0:T(8,128)(2,1)S(1)} %fusion.46.refs_0_), custom_call_target="tpu_custom_call" | custom-call | flops 20000000000 | bytes 1572864 | tf_op jit(solution)/shard_map/half_n1/pallas_call | solution.py:151
  343.8 2.1 slice.427
  351.4 2.3 slice.424
  357.0 12.7 %half_mixed.1 = bf16[4,64,1536]{2,1,0:T(8,128)(2,1)S(1)} custom-call(bf16[4,64,1536]{2,1,0:T(8,128)(2,1)S(1)} %bitcast.557), custom_call_target="tpu_custom_call" | custom-call | flops 20000000000 | bytes 1572864 | tf_op jit(solution)/shard_map/half_mixed/pallas_call | solution.py:151
  376.7 61.7 %spread_1.1 = (bf16[64,8,1536]{2,1,0:T(8,128)(2,1)S(1)}, bf16[64,8,1536]{2,1,0:T(8,128)(2,1)S(1)}, bf16[4,64,1536]{2,1,0:T(8,128)(2,1)S(1)}, bf16[4,64,1536]{2,1,0:T(8,128)(2,1)S(1)}) custom-call(bf16[64,8,1536]{2,1,0:T(8,128)(2,1)} %fusion.32.refs_0_, bf16[64,8,1536]{2,1,0:T(8,128)(2,1)} %fusion.36.refs_1_, ...), custom_call_target="tpu_custom_call" | custom-call | flops 80000000000 | bytes 9437184 | tf_op jit(solution)/shard_map/spread_1/pallas_call | solution.py:151
  444.0 2.8 fusion.179
  446.8 4.5 fusion.34.refs_0_
  451.9 4.9 fusion.30.refs_1_
  456.8 61.7 %collect_1.1 = (bf16[64,8,1536]{2,1,0:T(8,128)(2,1)S(1)}, bf16[64,8,1536]{2,1,0:T(8,128)(2,1)}, bf16[4,64,1536]{2,1,0:T(8,128)(2,1)S(1)}, bf16[4,64,1536]{2,1,0:T(8,128)(2,1)S(1)}) custom-call(bf16[64,8,1536]{2,1,0:T(8,128)(2,1)} %fusion.34.refs_0_, bf16[64,8,1536]{2,1,0:T(8,128)(2,1)} %fusion.30.refs_1_, bf16[4,64,1536]{2,1,0:T(8,128)(2,1)S(1)} %bitcast.565, ...), custom_call_target="tpu_custom_call" | custom-call | flops 80000000000 | bytes 9437184 | tf_op jit(solution)/shard_map/collect_1/pallas_call | solution.py:151
  523.0 13.3 %half_dmixed.1 = bf16[4,64,1536]{2,1,0:T(8,128)(2,1)S(1)} custom-call(bf16[64,1536]{1,0:T(8,128)(2,1)S(1)} %fusion.259.refs_0_), custom_call_target="tpu_custom_call" | custom-call | flops 20000000000 | bytes 1572864 | tf_op jit(solution)/shard_map/half_dmixed/pallas_call | solution.py:151
  546.5 2.1 reshape.833
  551.9 3.4 reshape.837
  557.4 3.6 pad_maximum_fusion
  561.0 2.4 convolution_convert_fusion.13
  563.4 13.7 %half_dn1.1 = bf16[4,64,1536]{2,1,0:T(8,128)(2,1)S(1)} custom-call(bf16[4,64,1536]{2,1,0:T(8,128)(2,1)S(1)} %bitcast.580), custom_call_target="tpu_custom_call" | custom-call | flops 20000000000 | bytes 1572864 | tf_op jit(solution)/shard_map/half_dn1/pallas_call | solution.py:151
  577.8 2.0 fusion.1
  582.9 34.0 %spread_back_0.1 = (bf16[64,8,1536]{2,1,0:T(8,128)(2,1)S(1)}, bf16[4,64,1536]{2,1,0:T(8,128)(2,1)S(1)}) custom-call(bf16[64,8,1536]{2,1,0:T(8,128)(2,1)S(1)} %fusion.35.refs_0_, bf16[64,1536]{1,0:T(8,128)(2,1)S(1)} %get-tuple-element.208.refs_1_), custom_call_target="tpu_custom_call" | custom-call | flops 40000000000 | bytes 4718592 | tf_op jit(solution)/shard_map/spread_back_0/pallas_call | solution.py:151
  617.0 2.2 convolution_convert_fusion.2
  623.4 3.5 convolution_convert_fusion
  633.9 32.1 %collect_back_0.1 = (bf16[64,8,1536]{2,1,0:T(8,128)(2,1)S(1)}, bf16[4,64,1536]{2,1,0:T(8,128)(2,1)S(1)}) custom-call(bf16[64,8,1536]{2,1,0:T(8,128)(2,1)S(1)} %bitcast.578, bf16[4,64,1536]{2,1,0:T(8,128)(2,1)S(1)} %bitcast.567), custom_call_target="tpu_custom_call" | custom-call | flops 40000000000 | bytes 4718592 | tf_op jit(solution)/shard_map/collect_back_0/pallas_call | solution.py:151
  668.4 2.9 collective-permute-start.7
  673.4 1.9 copy.394
  675.3 1.9 stack.115
  677.2 1.9 copy.395
  679.1 2.0 stack.116
  687.5 2.0 fusion.265
  691.1 2.7 fusion.51
  697.2 2.0 copy.400
  699.1 9.1 collective-permute-done.7
  708.9 35.3 %team_dmixed.1 = (bf16[96,512]{1,0:T(8,128)(2,1)S(1)}, bf16[16,1536]{1,0:T(8,128)(2,1)S(1)}, bf16[8,64,1536]{2,1,0:T(8,128)(2,1)S(1)}, f32[8,8,128]{2,1,0:T(8,128)S(1)}) custom-call(bf16[8,2,96,512]{3,2,1,0:T(8,128)(2,1)S(1)} %bitcast.553, bf16[8,2,16,1536]{3,2,1,0:T(8,128)(2,1)S(1)} %bitcast.564, bf16[64,1536]{1,0:T(8,128)(2,1)S(1)} %get-tuple-element.156.refs_2_, ...), custom_call_target="tpu_custom_call" | custom-call | flops 44999999488 | bytes 3506176 | tf_op jit(solution)/shard_map/team_dmixed/pallas_call | solution.py:151
  746.5 13.8 %mamba_backward.1 = (bf16[8,64,1152]{2,1,0:T(8,128)(2,1)S(1)}, bf16[8,64,384]{2,1,0:T(8,128)(2,1)S(1)}, f32[16,640]{1,0:T(8,128)S(1)}) custom-call(f32[8,64,1152]{2,1,0:T(8,128)S(1)} %copy-done.7, f32[8,64,64]{2,1,0:T(8,128)S(1)} %and_convert_fusion.masks_ref, f32[8,64,128]{2,1,0:T(8,128)S(1)} %copy-done.15, f32[8,640]{1,0:T(8,128)S(1)} %copy-done.32, ...), custom_call_target="tpu_custom_call" | custom-call | tf_op jit(solution)/shard_map/mamba_backward/pallas_call | solution.py:684
  762.3 6.4 fusion.12
  776.8 4.2 fusion.5
  781.0 7.1 collective-permute-done.9
  789.7 3.6 add_bitcast_fusion.1
  793.3 6.8 collective-permute-done.10
  801.8 64.7 %rank_grads.1 = (bf16[96,1152]{1,0:T(8,128)(2,1)S(1)}, bf16[32,1536]{1,0:T(8,128)(2,1)S(1)}, bf16[128,128]{1,0:T(8,128)(2,1)S(1)}, bf16[8,64,1536]{2,1,0:T(8,128)(2,1)S(1)}, bf16[2,64,1536]{2,1,0:T(8,128)(2,1)S(1)}) custom-call(bf16[8,2,96,1152]{3,2,1,0:T(8,128)(2,1)} %bitcast.675, bf16[8,2,32,1536]{3,2,1,0:T(8,128)(2,1)S(1)} %bitcast.550, ...), custom_call_target="tpu_custom_call" | custom-call | flops 44999999488 | bytes 4636672 | tf_op jit(solution)/shard_map/rank_grads/pallas_call | solution.py:151
  867.2 2.0 fusion
  871.9 17.9 %team_end.1 = (bf16[8,16,1152]{2,1,0:T(8,128)(2,1)S(1)}, bf16[8,16,640]{2,1,0:T(8,128)(2,1)S(1)}, bf16[8,32,512]{2,1,0:T(8,128)(2,1)S(1)}, bf16[2,16,1536]{2,1,0...) custom-call(bf16[8,16,1152]{2,1,0:T(8,128)(2,1)S(1)} %pad.144.refs_0, ...), custom_call_target="tpu_custom_call" | custom-call | flops 20000000000 | bytes 3473408 | tf_op jit(solution)/shard_map/team_end/pallas_call | solution.py:151
  899.7 8.2 add_bitcast_fusion
  (786 shorter events, 156.7 us)
Async XLA Ops:
  7.2 46.0 %copy-start = (s32[2,64,6]{1,0,2:T(2,128)S(1)}, s32[2,64,6]{1,0,2:T(2,128)}, u32[]{:S(2)}) copy-start(s32[2,64,6]{1,0,2:T(2,128)} %param.24) | copy-start | bytes 9220
  7.3 335.0 %all-gather.7.cloned.1.call-start = ((), (), s32[]{:S(2)}) async-start(), calls=%async_computation.2 | async-start | bytes 2088960 | tf_op jit(solution)/shard_map/all_gather | solution.py:811
  7.3 48.3 %collective-permute-start = (bf16[512,1536]{1,0:T(8,128)(2,1)}, bf16[512,1536]{1,0:T(8,128)(2,1)}, u32[]{:S(2)}, u32[]{:S(2)}) collective-permute-start(bf16[512,1536]{1,0:T(8,128)(2,1)} %bitcast.672), channel_id=1, source_target_pairs={{0,64},{64,0},{1,65},{65,1},{2,66},{66,2},{3,67},{67,3},{4,68},{68... | collective-permute-start | bytes 4718600 | tf_op jit(solution)/shard_map/ppermute | solution.py:784
  13.2 39.2 %copy-start.147 = (bf16[12,1536]{1,0:T(8,128)(2,1)S(1)}, bf16[12,1536]{1,0:T(8,128)(2,1)}, u32[]{:S(2)}) copy-start(bf16[12,1536]{1,0:T(8,128)(2,1)} %param.33) | copy-start | bytes 110596
  13.3 39.2 %copy-start.153 = (bf16[12,1024]{1,0:T(8,128)(2,1)S(1)}, bf16[12,1024]{1,0:T(8,128)(2,1)}, u32[]{:S(2)}) copy-start(bf16[12,1024]{1,0:T(8,128)(2,1)} %param.34) | copy-start | bytes 73732
  53.4 67.5 %copy-start.169 = (s32[1536]{0:T(1024)}, s32[1536]{0:T(1024)S(1)}, u32[]{:S(2)}) copy-start(s32[1536]{0:T(1024)S(1)} %fusion.209) | copy-start | bytes 18436
  55.6 37.5 %copy-start.212 = (f32[48]{0:T(128)S(1)}, f32[48]{0:T(128)}, u32[]{:S(2)}) copy-start(f32[48]{0:T(128)} %param.30) | copy-start | bytes 580
  55.6 39.5 %copy-start.198 = (f32[48]{0:T(128)S(1)}, f32[48]{0:T(128)}, u32[]{:S(2)}) copy-start(f32[48]{0:T(128)} %param.29) | copy-start | bytes 580
  55.6 39.5 %copy-start.199 = (f32[48]{0:T(128)S(1)}, f32[48]{0:T(128)}, u32[]{:S(2)}) copy-start(f32[48]{0:T(128)} %param.28) | copy-start | bytes 580
  92.2 113.5 %copy-start.8 = (bf16[8,64,1536]{2,1,0:T(8,128)(2,1)}, bf16[8,64,1536]{2,1,0:T(8,128)(2,1)S(1)}, u32[]{:S(2)}) copy-start(bf16[8,64,1536]{2,1,0:T(8,128)(2,1)S(1)} %get-tuple-element.113) | copy-start | bytes 4718596
  93.0 256.7 %all-gather.5.cloned.1.call-start = ((), (), s32[]{:S(2)}) async-start(), calls=%async_computation.1 | async-start | bytes 3760128 | tf_op jit(solution)/shard_map/all_gather | solution.py:810
  93.6 279.4 %copy-start.111 = (pred[64,64]{0,1:T(32,128)(4,1)}, pred[64,64]{0,1:T(32,128)(4,1)S(1)}, u32[]{:S(2)}) copy-start(pred[64,64]{0,1:T(32,128)(4,1)S(1)} %copy.382) | copy-start | bytes 12292
  95.3 77.3 %copy-start.33 = (f32[8,128]{1,0:T(8,128)}, f32[8,128]{1,0:T(8,128)S(1)}, u32[]{:S(2)}) copy-start(f32[8,128]{1,0:T(8,128)S(1)} %select_maximum_fusion.1.heads_ref) | copy-start | bytes 12292
  95.3 77.3 %copy-start.14 = (f32[8,64,128]{2,1,0:T(8,128)}, f32[8,64,128]{2,1,0:T(8,128)S(1)}, u32[]{:S(2)}) copy-start(f32[8,64,128]{2,1,0:T(8,128)S(1)} %pad_convert_fusion.same_ref) | copy-start | bytes 786436
  95.8 278.4 %copy-start.79 = (pred[64,512]{1,0:T(32,128)(4,1)}, pred[64,512]{1,0:T(32,128)(4,1)S(1)}, u32[]{:S(2)}) copy-start(pred[64,512]{1,0:T(32,128)(4,1)S(1)} %convolution_compare_fusion) | copy-start | bytes 98308
  104.3 15.9 %collective-permute-start.1 = (bf16[256,1024]{1,0:T(8,128)(2,1)}, bf16[256,1024]{1,0:T(8,128)(2,1)}, u32[]{:S(2)}, u32[]{:S(2)}) collective-permute-start(bf16[256,1024]{1,0:T(8,128)(2,1)} %get-tuple-element.234), channel_id=1, source_target_pairs={{0,64},{64,0},{1,65},{65,1},{2,66},{66,2},{3,67},{67,3},{4,68},{68... | collective-permute-start | bytes 1572872 | tf_op jit(solution)/shard_map/ppermute | solution.py:784
  105.9 17.8 %copy-start.133 = (f32[1536]{0:T(1024)}, f32[1536]{0:T(1024)S(1)}, u32[]{:S(2)}) copy-start(f32[1536]{0:T(1024)S(1)} %get-tuple-element.204) | copy-start | bytes 18436
  105.9 186.1 %copy-start.126 = (f32[1536]{0:T(1024)}, f32[1536]{0:T(1024)S(1)}, u32[]{:S(2)}) copy-start(f32[1536]{0:T(1024)S(1)} %get-tuple-element.203) | copy-start | bytes 18436
  120.2 19.1 %collective-permute-start.2 = (bf16[256,1024]{1,0:T(8,128)(2,1)}, bf16[256,1024]{1,0:T(8,128)(2,1)}, u32[]{:S(2)}, u32[]{:S(2)}) collective-permute-start(bf16[256,1024]{1,0:T(8,128)(2,1)} %get-tuple-element.111), channel_id=1, source_target_pairs={{0,64},{64,0},{1,65},{65,1},{2,66},{66,2},{3,67},{67,3},{4,68},{68... | collective-permute-start | bytes 1572872 | tf_op jit(solution)/shard_map/ppermute | solution.py:784
  126.7 41.3 %copy-start.167 = (f32[1536]{0:T(1024)}, f32[1536]{0:T(1024)S(1)}, u32[]{:S(2)}) copy-start(f32[1536]{0:T(1024)S(1)} %convert_element_type.678) | copy-start | bytes 18436
  132.5 159.5 %copy-start.66 = (bf16[1,4,16,24,64]{4,3,2,1,0:T(8,128)(2,1)}, bf16[1,4,16,24,64]{4,3,2,1,0:T(8,128)(2,1)S(1)}, u32[]{:S(2)}) copy-start(bf16[1,4,16,24,64]{4,3,2,1,0:T(8,128)(2,1)S(1)} %copy.371) | copy-start | bytes 589828
  139.4 11.2 %collective-permute-start.3 = (bf16[256,1024]{1,0:T(8,128)(2,1)}, bf16[256,1024]{1,0:T(8,128)(2,1)}, u32[]{:S(2)}, u32[]{:S(2)}) collective-permute-start(bf16[256,1024]{1,0:T(8,128)(2,1)} %get-tuple-element.112), channel_id=1, source_target_pairs={{0,64},{64,0},{1,65},{65,1},{2,66},{66,2},{3,67},{67,3},{4,68},{68... | collective-permute-start | bytes 1572872 | tf_op jit(solution)/shard_map/ppermute | solution.py:784
  140.7 659.4 %reduce-scatter.4.cloned.1.call-start = ((), (), s32[]{:S(2)}) async-start(), calls=%async_computation.3 | async-start | bytes 5953536
  140.9 31.7 %copy-start.31 = (f32[8,640]{1,0:T(8,128)}, f32[8,640]{1,0:T(8,128)S(1)}, u32[]{:S(2)}) copy-start(f32[8,640]{1,0:T(8,128)S(1)} %maximum_maximum_fusion.taps_ref) | copy-start | bytes 61444
  152.0 16.0 %copy-start.213 = (bf16[16,96,1152]{2,1,0:T(8,128)(2,1)S(1)}, bf16[16,96,1152]{2,1,0:T(8,128)(2,1)}, u32[]{:S(2)}) copy-start(bf16[16,96,1152]{2,1,0:T(8,128)(2,1)} %get-tuple-element.115) | copy-start | bytes 10616836
  152.0 30.9 %collective-permute-start.4 = (bf16[256,1024]{1,0:T(8,128)(2,1)S(1)}, bf16[256,1024]{1,0:T(8,128)(2,1)S(1)}, u32[]{:S(2)}, u32[]{:S(2)}) collective-permute-start(bf16[256,1024]{1,0:T(8,128)(2,1)S(1)} %get-tuple-element.231), channel_id=1, source_target_pairs={{0,64},{64,0},{1,65},{65,1},{2,66},{66,2},{3,67},{67,3},{4,68},{68... | collective-permute-start | bytes 1572872 | tf_op jit(solution)/shard_map/ppermute | solution.py:784
  164.2 41.5 %copy-start.158 = (f32[8,64]{1,0:T(8,128)}, f32[8,64]{1,0:T(8,128)S(1)}, u32[]{:S(2)}) copy-start(f32[8,64]{1,0:T(8,128)S(1)} %add_rsqrt_fusion) | copy-start | bytes 6148
  182.9 22.1 %collective-permute-start.5 = (bf16[256,1024]{1,0:T(8,128)(2,1)S(1)}, bf16[256,1024]{1,0:T(8,128)(2,1)S(1)}, u32[]{:S(2)}, u32[]{:S(2)}) collective-permute-start(bf16[256,1024]{1,0:T(8,128)(2,1)S(1)} %get-tuple-element.123), channel_id=1, source_target_pairs={{0,64},{64,0},{1,65},{65,1},{2,66},{66,2},{3,67},{67,3},{4,68},{68... | collective-permute-start | bytes 1572872 | tf_op jit(solution)/shard_map/ppermute | solution.py:784
  205.0 9.2 %collective-permute-start.6 = (bf16[256,1024]{1,0:T(8,128)(2,1)S(1)}, bf16[256,1024]{1,0:T(8,128)(2,1)S(1)}, u32[]{:S(2)}, u32[]{:S(2)}) collective-permute-start(bf16[256,1024]{1,0:T(8,128)(2,1)S(1)} %get-tuple-element.124), channel_id=1, source_target_pairs={{0,64},{64,0},{1,65},{65,1},{2,66},{66,2},{3,67},{67,3},{4,68},{68... | collective-permute-start | bytes 1572872 | tf_op jit(solution)/shard_map/ppermute | solution.py:784
  237.2 55.3 %copy-start.25 = (bf16[16,16,1536]{2,1,0:T(8,128)(2,1)}, bf16[16,16,1536]{2,1,0:T(8,128)(2,1)S(1)}, u32[]{:S(2)}) copy-start(bf16[16,16,1536]{2,1,0:T(8,128)(2,1)S(1)} %get-tuple-element.137) | copy-start | bytes 2359300
  237.4 54.6 %copy-start.58 = (f32[64,1536]{1,0:T(8,128)}, f32[64,1536]{1,0:T(8,128)S(1)}, u32[]{:S(2)}) copy-start(f32[64,1536]{1,0:T(8,128)S(1)} %convert_reduce_fusion.1) | copy-start | bytes 1179652
  238.0 54.1 %copy-start.178 = (f32[64]{0:T(128)}, f32[64]{0:T(128)S(1)}, u32[]{:S(2)}) copy-start(f32[64]{0:T(128)S(1)} %get-tuple-element.259) | copy-start | bytes 772
  238.7 39.2 %copy-start.194 = (f32[64]{0:T(128)}, f32[64]{0:T(128)S(1)}, u32[]{:S(2)}) copy-start(f32[64]{0:T(128)S(1)} %get-tuple-element.215) | copy-start | bytes 772
  238.7 86.7 %copy-start.51 = (f32[64,1536]{1,0:T(8,128)}, f32[64,1536]{1,0:T(8,128)S(1)}, u32[]{:S(2)}) copy-start(f32[64,1536]{1,0:T(8,128)S(1)} %get-tuple-element.216) | copy-start | bytes 1179652
  238.7 53.3 %copy-start.162 = (f32[64]{0:T(128)}, f32[64]{0:T(128)S(1)}, u32[]{:S(2)}) copy-start(f32[64]{0:T(128)S(1)} %fusion.235) | copy-start | bytes 772
  238.8 39.0 %copy-start.16 = (bf16[64,1536]{1,0:T(8,128)(2,1)}, bf16[64,1536]{1,0:T(8,128)(2,1)S(1)}, u32[]{:S(2)}) copy-start(bf16[64,1536]{1,0:T(8,128)(2,1)S(1)} %multiply_convert_fusion.6.refs_1_) | copy-start | bytes 589828
  292.4 31.5 %copy-start.115 = (f32[64,64]{0,1:T(8,128)}, f32[64,64]{0,1:T(8,128)S(1)}, u32[]{:S(2)}) copy-start(f32[64,64]{0,1:T(8,128)S(1)} %get-tuple-element.261) | copy-start | bytes 49156
  292.4 31.5 %copy-start.173 = (f32[64]{0:T(128)}, f32[64]{0:T(128)S(1)}, u32[]{:S(2)}) copy-start(f32[64]{0:T(128)S(1)} %get-tuple-element.260) | copy-start | bytes 772
  292.4 31.4 %copy-start.180 = (f32[64]{0:T(128)}, f32[64]{0:T(128)S(1)}, u32[]{:S(2)}) copy-start(f32[64]{0:T(128)S(1)} %fusion.195) | copy-start | bytes 772
  292.8 31.0 %copy-start.189 = (s32[512]{0:T(512)S(1)}, s32[512]{0:T(512)}, u32[]{:S(2)}) copy-start(s32[512]{0:T(512)} %copy-done.188) | copy-start | bytes 6148
  325.9 44.0 %copy-start.60 = (bf16[64,1536]{1,0:T(8,128)(2,1)}, bf16[64,1536]{1,0:T(8,128)(2,1)S(1)}, u32[]{:S(2)}) copy-start(bf16[64,1536]{1,0:T(8,128)(2,1)S(1)} %get-tuple-element.263) | copy-start | bytes 589828
  342.2 11.5 %copy-start.38 = (bf16[4,64,1536]{2,1,0:T(8,128)(2,1)}, bf16[4,64,1536]{2,1,0:T(8,128)(2,1)S(1)}, u32[]{:S(2)}) copy-start(bf16[4,64,1536]{2,1,0:T(8,128)(2,1)S(1)} %half_n1.1) | copy-start | bytes 2359300
  356.4 13.4 %copy-start.89 = (bf16[4,64,3,128]{3,2,1,0:T(4,128)(2,1)}, bf16[4,64,3,128]{3,2,1,0:T(4,128)(2,1)S(1)}, u32[]{:S(2)}) copy-start(bf16[4,64,3,128]{3,2,1,0:T(4,128)(2,1)S(1)} %copy.377) | copy-start | bytes 589828
  376.7 64.3 %copy-start.138 = (bf16[1,1,1536,1024]{3,2,1,0:T(8,128)(2,1)S(1)}, bf16[1,1,1536,1024]{3,2,1,0:T(8,128)(2,1)}, u32[]{:S(2)}) copy-start(bf16[1,1,1536,1024]{3,2,1,0:T(8,128)(2,1)} %copy-done.137) | copy-start | bytes 9437188
  456.8 61.8 %copy-start.80 = (pred[64,512]{1,0:T(32,128)(4,1)S(1)}, pred[64,512]{1,0:T(32,128)(4,1)}, u32[]{:S(2)}) copy-start(pred[64,512]{1,0:T(32,128)(4,1)} %copy-done.79) | copy-start | bytes 98308
  523.0 13.4 %copy-start.64 = (bf16[3,128,1536,1]{2,1,0,3:T(8,128)(2,1)S(1)}, bf16[3,128,1536,1]{2,1,0,3:T(8,128)(2,1)}, u32[]{:S(2)}) copy-start(bf16[3,128,1536,1]{2,1,0,3:T(8,128)(2,1)} %reshape.894) | copy-start | bytes 3538948
  582.9 34.0 %copy-start.20 = (bf16[64,8,1536]{2,1,0:T(8,128)(2,1)S(1)}, bf16[64,8,1536]{2,1,0:T(8,128)(2,1)}, u32[]{:S(2)}) copy-start(bf16[64,8,1536]{2,1,0:T(8,128)(2,1)} %copy-done.19) | copy-start | bytes 4718596
  582.9 34.0 %copy-start.86 = (bf16[512,512]{1,0:T(8,128)(2,1)S(1)}, bf16[512,512]{1,0:T(8,128)(2,1)}, u32[]{:S(2)}) copy-start(bf16[512,512]{1,0:T(8,128)(2,1)} %copy-done.85) | copy-start | bytes 1572868
  582.9 34.0 %copy-start.122 = (bf16[512,512]{1,0:T(8,128)(2,1)S(1)}, bf16[512,512]{1,0:T(8,128)(2,1)}, u32[]{:S(2)}) copy-start(bf16[512,512]{1,0:T(8,128)(2,1)} %copy-done.121) | copy-start | bytes 1572868
  616.9 14.8 %copy-start.27 = (bf16[4,64,1536]{2,1,0:T(8,128)(2,1)}, bf16[4,64,1536]{2,1,0:T(8,128)(2,1)S(1)}, u32[]{:S(2)}) copy-start(bf16[4,64,1536]{2,1,0:T(8,128)(2,1)S(1)} %get-tuple-element.150) | copy-start | bytes 2359300
  632.1 33.8 %copy-start.101 = (f32[256,256]{1,0:T(8,128)}, f32[256,256]{1,0:T(8,128)S(1)}, u32[]{:S(2)}) copy-start(f32[256,256]{1,0:T(8,128)S(1)} %get-tuple-element.235) | copy-start | bytes 786436
  632.2 33.8 %copy-start.103 = (f32[256,256]{1,0:T(8,128)}, f32[256,256]{1,0:T(8,128)S(1)}, u32[]{:S(2)}) copy-start(f32[256,256]{1,0:T(8,128)S(1)} %get-tuple-element.236) | copy-start | bytes 786436
  633.8 32.2 %copy-start.52 = (f32[64,1536]{1,0:T(8,128)S(1)}, f32[64,1536]{1,0:T(8,128)}, u32[]{:S(2)}) copy-start(f32[64,1536]{1,0:T(8,128)} %copy-done.51) | copy-start | bytes 1179652
  633.9 32.2 %copy-start.127 = (f32[1536]{0:T(1024)S(1)}, f32[1536]{0:T(1024)}, u32[]{:S(2)}) copy-start(f32[1536]{0:T(1024)} %copy-done.126) | copy-start | bytes 18436
  633.9 32.2 %copy-start.163 = (f32[64]{0:T(128)S(1)}, f32[64]{0:T(128)}, u32[]{:S(2)}) copy-start(f32[64]{0:T(128)} %copy-done.162) | copy-start | bytes 772
  668.4 39.8 %collective-permute-start.7 = (bf16[512,1536]{1,0:T(8,128)(2,1)}, bf16[512,1536]{1,0:T(8,128)(2,1)}, u32[]{:S(2)}, u32[]{:S(2)}) collective-permute-start(bf16[512,1536]{1,0:T(8,128)(2,1)} %convolution_convert_fusion.2), channel_id=1, source_target_pairs={{0,64},{64,0},{1,65},{65,1},{2,66},{66,2},{3,67},{67,3},{4,68},{68... | collective-permute-start | bytes 4718600 | tf_op jit(solution)/shard_map/ppermute | solution.py:784
  708.9 35.3 %copy-start.63 = (bf16[16,24,1536]{2,1,0:T(8,128)(2,1)S(1)}, bf16[16,24,1536]{2,1,0:T(8,128)(2,1)}, u32[]{:S(2)}) copy-start(bf16[16,24,1536]{2,1,0:T(8,128)(2,1)} %slice.335) | copy-start | bytes 3538948
  746.5 13.8 %copy-start.57 = (bf16[768,1024]{1,0:T(8,128)(2,1)S(1)}, bf16[768,1024]{1,0:T(8,128)(2,1)}, u32[]{:S(2)}) copy-start(bf16[768,1024]{1,0:T(8,128)(2,1)} %get-tuple-element.164) | copy-start | bytes 4718596
  761.6 13.5 %collective-permute-start.8 = (bf16[256,1024]{1,0:T(8,128)(2,1)}, bf16[256,1024]{1,0:T(8,128)(2,1)}, u32[]{:S(2)}, u32[]{:S(2)}) collective-permute-start(bf16[256,1024]{1,0:T(8,128)(2,1)} %get-tuple-element.228), channel_id=1, source_target_pairs={{0,64},{64,0},{1,65},{65,1},{2,66},{66,2},{3,67},{67,3},{4,68},{68... | collective-permute-start | bytes 1572872 | tf_op jit(solution)/shard_map/ppermute | solution.py:784
  775.1 13.0 %copy-start.119 = (bf16[256,1024]{1,0:T(8,128)(2,1)S(1)}, bf16[256,1024]{1,0:T(8,128)(2,1)}, u32[]{:S(2)}) copy-start(bf16[256,1024]{1,0:T(8,128)(2,1)} %get-tuple-element.166) | copy-start | bytes 1572868
  775.1 13.0 %collective-permute-start.9 = (bf16[256,1024]{1,0:T(8,128)(2,1)S(1)}, bf16[256,1024]{1,0:T(8,128)(2,1)S(1)}, u32[]{:S(2)}, u32[]{:S(2)}) collective-permute-start(bf16[256,1024]{1,0:T(8,128)(2,1)S(1)} %copy-done.120), channel_id=1, source_target_pairs={{0,64},{64,0},{1,65},{65,1},{2,66},{66,2},{3,67},{67,3},{4,68},{68... | collective-permute-start | bytes 1572872 | tf_op jit(solution)/shard_map/ppermute | solution.py:784
  776.8 12.9 %copy-start.55 = (f32[512,1536]{1,0:T(8,128)S(1)}, f32[512,1536]{1,0:T(8,128)}, u32[]{:S(2)}) copy-start(f32[512,1536]{1,0:T(8,128)} %fusion.51) | copy-start | bytes 9437188
  788.1 12.0 %collective-permute-start.10 = (bf16[256,1024]{1,0:T(8,128)(2,1)S(1)}, bf16[256,1024]{1,0:T(8,128)(2,1)}, u32[]{:S(2)}, u32[]{:S(2)}) collective-permute-start(bf16[256,1024]{1,0:T(8,128)(2,1)S(1)} %copy-done.119), channel_id=1, source_target_pairs={{0,64},{64,0},{1,65},{65,1},{2,66},{66,2},{3,67},{67,3},{4,68},{68... | collective-permute-start | bytes 1572872 | tf_op jit(solution)/shard_map/ppermute | solution.py:784
  800.1 71.7 %collective-permute-start.11 = (bf16[768,1024]{1,0:T(8,128)(2,1)}, bf16[768,1024]{1,0:T(8,128)(2,1)}, u32[]{:S(2)}, u32[]{:S(2)}) collective-permute-start(bf16[768,1024]{1,0:T(8,128)(2,1)} %get-tuple-element.172), channel_id=1, source_target_pairs={{0,64},{64,0},{1,65},{65,1},{2,66},{66,2},{3,67},{67,3},{4,68},{68... | collective-permute-start | bytes 4718600 | tf_op jit(solution)/shard_map/ppermute | solution.py:784
  (177 other events, 470.7 us)
Sparse Core Ops, SparseCore 0:
  93.1 55.9 all-gather.6
  152.1 61.5 all-gather.4
  671.5 96.5 reduce-scatter.3
